TPU v7x, 32 devices: a whole 2x2x4 slice. The times are simulated.
32 devices in a mesh: feat: 16 (over z, y, x), rep: 2 (over core).
Axes of the slice: x: 2, y: 2, z: 4, core: 2. Of those that a mesh axis runs over, the one named last changes fastest.
Arguments:
- features: bfloat16 [2048, 10, 2048], P('feat', 'rep'), may hold values from -6 to 6
- adjacency: bfloat16 [10, 2048, 2048], P('rep'), may hold values from 0 to 1, as said below
- counts: int32 [10], P('rep'), may hold values from 600 to 2048, as said below
- weight: bfloat16 [2048, 2048], replicated, may hold values from -0.125 to 0.125
- bias: bfloat16 [2048], replicated, may hold values from -3 to 3
- cotangent: bfloat16 [2048, 10, 2048], P('feat', 'rep'), may hold values from -6 to 6
Outputs:
- activations: float32 [2048, 10, 2048], P('feat', 'rep')
- grad_features: float32 [2048, 10, 2048], P('feat', 'rep')
- grad_weight: float32 [2048, 2048], replicated
- grad_bias: float32 [2048], replicated
Inputs may be any that keep to these rules, and one draw needn't show every extreme that they name: `counts`: every index of rep holds 5 clusters, one of which has all 2048 nodes live. `adjacency`: Nonnegative; rows and columns of slots at or beyond a cluster's count are zero.
All inputs are finite; a program needn't handle non-finite values.
Results may differ from a plain program's by a relative error of at most 0.005.
Values may be sent and summed in bfloat16 or wider, within the bound.
No kernel may reach another device: no remote copies, remote signals or barrier semaphores. Data moves between devices by JAX's collectives and lax.ppermute only.
A program may use at most 256 MiB of HBM per device.

v0:
```python
import jax
import jax.numpy as jnp
from jax import lax
from jax.sharding import PartitionSpec as P


def gelu_piece(values):
    return jax.nn.gelu(values, approximate=False)


def local(features, adjacency, counts, weight, bias, cotangent):
    feat_count = lax.axis_size("feat")
    position = lax.axis_index("feat")
    clusters = features.shape[1]
    nodes = features.shape[2]
    slots = lax.broadcasted_iota(jnp.int32, (clusters, nodes), 1)
    mask = (slots < counts[:, None]).astype(jnp.float32)
    masked = features * mask[None].astype(jnp.bfloat16)
    diagonal = jnp.diagonal(adjacency, axis1=1, axis2=2).astype(jnp.float32)
    aggregated = jnp.einsum("fcj,cij->fci", masked, adjacency, preferred_element_type=jnp.float32)
    aggregated = aggregated + diagonal[None] * masked.astype(jnp.float32)
    agg_low = aggregated.astype(jnp.bfloat16)
    row_count = nodes // feat_count
    row_mask = lax.dynamic_slice_in_dim(mask, position * row_count, row_count, 1)[None]
    agg_rows = lax.all_to_all(agg_low, "feat", split_axis=2, concat_axis=0, tiled=True)
    pre = jnp.einsum("fg,fcr->gcr", weight, agg_rows, preferred_element_type=jnp.float32)
    pre = pre + bias.astype(jnp.float32)[:, None, None]
    result, pullback = jax.vjp(gelu_piece, pre)
    activations = lax.all_to_all(row_mask * result, "feat", split_axis=0, concat_axis=2, tiled=True)
    incoming = lax.all_to_all(cotangent, "feat", split_axis=2, concat_axis=0, tiled=True)
    grad_pre = pullback(row_mask * incoming.astype(jnp.float32))[0]
    grad_low = grad_pre.astype(jnp.bfloat16)
    weight_part = jnp.einsum("fcr,gcr->fg", agg_rows, grad_low, preferred_element_type=jnp.float32)
    bias_part = jnp.sum(grad_pre, axis=(1, 2))
    grad_weight, grad_bias = lax.psum((weight_part, bias_part), ("feat", "rep"))
    grad_rows = jnp.einsum(
        "fg,gcr->fcr", weight, grad_low, preferred_element_type=jnp.float32
    ).astype(jnp.bfloat16)
    grad_agg = lax.all_to_all(grad_rows, "feat", split_axis=0, concat_axis=2, tiled=True)
    spread = jnp.einsum("fci,cij->fcj", grad_agg, adjacency, preferred_element_type=jnp.float32)
    spread = spread + diagonal[None] * grad_agg.astype(jnp.float32)
    grad_features = mask[None] * spread
    return (activations, grad_features, grad_weight, grad_bias)


def solution(mesh):
    placed = (
        P("feat", "rep", None),
        P("rep", None, None),
        P("rep"),
        P(),
        P(),
        P("feat", "rep", None),
    )
    return jax.shard_map(
        local,
        mesh=mesh,
        in_specs=placed,
        out_specs=(P("feat", "rep", None), P("feat", "rep", None), P(), P()),
        check_vma=False,
    )
```

profile of v0, /device:TPU:0, one launch (start us, length us, event | category | flops | bytes accessed | tf_op | source)
XLA Modules:
  0.0 931.7 jit_solution(14884037368936989634)
XLA Ops:
  7.2 0.7 fusion.37
  7.9 43.7 %copy.24 = bf16[5,2048,2048]{2,0,1:T(8,128)(2,1)} copy(bf16[5,2048,2048]{2,1,0:T(8,128)(2,1)} %param.7) | data formatting | bytes 83886080 | tf_op args[1]
  51.7 24.4 %gather_fusion = bf16[2048,5]{0,1:T(8,128)(2,1)S(1)} fusion(bf16[5,2048,2048]{2,0,1:T(8,128)(2,1)} %copy.24, s32[2048]{0:T(1024)S(1)} %bitcast.138), kind=kCustom, calls=%fused_computation | custom fusion | bytes 57344 | tf_op jit(solution)/shard_map/jit(diagonal)/gather | solution.py:19
  76.0 20.0 %fusion.13 = bf16[128,5,2048]{2,0,1:T(8,128)(2,1)S(1)} fusion(bf16[5,2048,2048]{2,1,0:T(8,128)(2,1)} %param.7, f32[5,2048]{1,0:T(8,128)S(1)} %convert_bitcast_fusion, bf16[128,5,2048]{2,0,1:T(8,128)(2,1)} %param.6, bf16[5,2048]{1,0:T(8,128)(2,1)S(1)} %get-tuple-element.7), kind=kOutput, calls=%fused_computation.24 | convolution fusion | flops 5376573440 | bytes 47247360 | tf_op jit(solution)/shard_map/fcj,cij->fci/dot_general | solution.py:20
  96.0 4.7 copy.25
  100.7 8.6 all-to-all-start
  109.3 4.7 copy.29
  114.0 75.1 %all-to-all-done = bf16[128,5,2048]{0,1,2:T(8,128)(2,1)} async-done(((bf16[128,5,2048]{0,1,2:T(8,128)(2,1)}), bf16[128,5,2048]{0,1,2:T(8,128)(2,1)}, u32[]{:S(2)}, u32[]{:S(2)}) %all-to-all-start) | async-done | bytes 2621472 | tf_op jit(solution)/shard_map/all_to_all | solution.py:25
  189.1 20.1 %all-to-all-start.2 = ((bf16[128,5,2048]{0,1,2:T(8,128)(2,1)}), bf16[128,5,2048]{0,1,2:T(8,128)(2,1)}, u32[]{:S(2)}, u32[]{:S(2)}) async-start(bf16[128,5,2048]{0,1,2:T(8,128)(2,1)} %copy.29), calls=%async_computation.2 | async-start | bytes 8388608 | tf_op jit(solution)/shard_map/all_to_all | solution.py:30
  209.2 4.1 copy.42
  213.3 3.1 all_to_all.49
  216.4 71.2 %all-to-all-done.2 = bf16[128,5,2048]{0,1,2:T(8,128)(2,1)} async-done(((bf16[128,5,2048]{0,1,2:T(8,128)(2,1)}), bf16[128,5,2048]{0,1,2:T(8,128)(2,1)}, u32[]{:S(2)}, u32[]{:S(2)}) %all-to-all-start.2) | async-done | bytes 2621472 | tf_op jit(solution)/shard_map/all_to_all | solution.py:30
  287.6 6.4 copy.40
  294.0 6.9 reshape.45
  300.8 21.6 %fusion.38 = (f32[2048]{0:T(1024)S(1)}, bf16[2048,5,128]{0,2,1:T(8,128)(2,1)S(1)}, f32[2048,5,128]{0,2,1:T(8,128)}, f32[5,128,2048]{2,1,0:T(8,128)}) fusion(f32[2048,5,128]{0,2,1:T(8,128)} %reshape.45, f32[5,128]{1,0:T(8,128)S(1)} %constant_dynamic-slice_fusion, f32[2048]{0:T(1024)S(1)} %convert_element_type.63, bf16[2048,5,128]{0,2,1:T(8,128)(2,1)S(1)} %copy-done.1, ...), kind=kOutput, calls=%fused_computation.53 | convolution fusion | flops 5467011072 | bytes 29379072 | tf_op jit(solution)/shard_map/fg,fcr->gcr/dot_general | solution.py:26
  322.4 1.5 copy-done.3
  323.9 10.3 %fusion.29 = bf16[2048,5,128]{0,2,1:T(8,128)(2,1)} fusion(bf16[2048,2048]{1,0:T(8,128)(2,1)} %param.9, bf16[2048,5,128]{0,2,1:T(8,128)(2,1)S(1)} %get-tuple-element.5), kind=kOutput, calls=%fused_computation.40 | convolution fusion | flops 5370019840 | bytes 13631488 | tf_op jit(solution)/shard_map/fg,gcr->fcr/dot_general | solution.py:36
  334.2 6.2 copy.31
  340.4 19.3 %all-to-all-start.3 = ((bf16[2048,5,128]{2,1,0:T(8,128)(2,1)}), bf16[2048,5,128]{2,1,0:T(8,128)(2,1)}, u32[]{:S(2)}, u32[]{:S(2)}) async-start(bf16[2048,5,128]{2,1,0:T(8,128)(2,1)} %copy.31), calls=%async_computation.3 | async-start | bytes 8388608 | tf_op jit(solution)/shard_map/all_to_all | solution.py:39
  359.7 7.2 fusion.7
  366.9 7.9 copy.27
  374.8 63.4 %all-to-all-done.3 = bf16[2048,5,128]{2,1,0:T(8,128)(2,1)} async-done(((bf16[2048,5,128]{2,1,0:T(8,128)(2,1)}), bf16[2048,5,128]{2,1,0:T(8,128)(2,1)}, u32[]{:S(2)}, u32[]{:S(2)}) %all-to-all-start.3) | async-done | bytes 2621472 | tf_op jit(solution)/shard_map/all_to_all | solution.py:39
  438.2 19.3 %all-to-all-start.1 = ((f32[2048,5,128]{2,1,0:T(8,128)}), f32[2048,5,128]{2,1,0:T(8,128)}, u32[]{:S(2)}, u32[]{:S(2)}) async-start(f32[2048,5,128]{2,1,0:T(8,128)} %copy.27), calls=%async_computation.1 | async-start | bytes 16777216 | tf_op jit(solution)/shard_map/all_to_all | solution.py:29
  457.5 12.1 %convolution_bitcast_fusion = f32[2048,2048]{1,0:T(8,128)} fusion(bf16[2048,5,128]{0,2,1:T(8,128)(2,1)S(1)} %copy-done.1, bf16[2048,5,128]{0,2,1:T(8,128)(2,1)} %copy-done.3), kind=kOutput, calls=%fused_computation.1 | convolution fusion | flops 5368709120 | bytes 22020096 | tf_op jit(solution)/shard_map/fcr,gcr->fg/dot_general | solution.py:33
  469.7 272.3 %psum.15 = f32[2048]{0:T(1024)} all-reduce(f32[2048]{0:T(1024)S(1)} %get-tuple-element.4), channel_id=1, replica_groups=mesh['feat'=16,'rep'=2] {'feat','rep'}, use_global_device_ids=true, to_apply=%region_2.3 | all-reduce | flops 2048 | bytes 16384 | tf_op jit(solution)/shard_map/psum | solution.py:35
  742.0 5.9 copy.41
  747.9 3.8 all_to_all.58
  751.7 18.9 %fusion.5 = f32[128,5,2048]{2,0,1:T(8,128)} fusion(bf16[128,5,2048]{2,0,1:T(8,128)(2,1)S(1)} %all_to_all.58, bf16[5,2048,2048]{2,1,0:T(8,128)(2,1)} %param.7, f32[5,2048]{1,0:T(8,128)S(1)} %get-tuple-element.8, f32[5,2048]{1,0:T(8,128)S(1)} %convert_bitcast_fusion), kind=kOutput, calls=%fused_computation.9 | convolution fusion | flops 5373952000 | bytes 49889280 | tf_op jit(solution)/shard_map/fci,cij->fcj/dot_general | solution.py:40
  770.6 8.9 copy.28
  779.5 6.8 all_to_all.53
  786.3 126.7 %all-reduce.2.cloned.1.call-done = f32[2048,2048]{1,0:T(8,128)} async-done(((f32[2048,2048]{1,0:T(8,128)}), f32[2048,2048]{1,0:T(8,128)}) %all-reduce.2.cloned.1.call-update) | async-done | bytes 16777232 | tf_op jit(solution)/shard_map/psum | solution.py:35
  913.0 11.8 %copy.44 = f32[2048,2048]{1,0:T(8,128)} copy(f32[2048,2048]{1,0:T(8,128)} %all-reduce.2.cloned.1.call-done) | data formatting | bytes 33554432
  (14 shorter events, 0.1 us)
Async XLA Ops:
  100.7 8.6 copy-start
  100.7 88.4 %all-to-all-start = ((bf16[128,5,2048]{0,1,2:T(8,128)(2,1)}), bf16[128,5,2048]{0,1,2:T(8,128)(2,1)}, u32[]{:S(2)}, u32[]{:S(2)}) async-start(bf16[128,5,2048]{0,1,2:T(8,128)(2,1)} %copy.25), calls=%async_computation | async-start | bytes 8388608 | tf_op jit(solution)/shard_map/all_to_all | solution.py:25
  114.0 95.1 %copy-start.2 = (bf16[2048]{0:T(1024)(128)(2,1)S(1)}, bf16[2048]{0:T(1024)(128)(2,1)}, u32[]{:S(2)}) copy-start(bf16[2048]{0:T(1024)(128)(2,1)} %param.10) | copy-start | bytes 12292
  189.1 98.5 %all-to-all-start.2 = ((bf16[128,5,2048]{0,1,2:T(8,128)(2,1)}), bf16[128,5,2048]{0,1,2:T(8,128)(2,1)}, u32[]{:S(2)}, u32[]{:S(2)}) async-start(bf16[128,5,2048]{0,1,2:T(8,128)(2,1)} %copy.29), calls=%async_computation.2 | async-start | bytes 8388608 | tf_op jit(solution)/shard_map/all_to_all | solution.py:30
  294.0 6.9 copy-start.1
  322.4 1.5 copy-start.3
  340.4 97.8 %all-to-all-start.3 = ((bf16[2048,5,128]{2,1,0:T(8,128)(2,1)}), bf16[2048,5,128]{2,1,0:T(8,128)(2,1)}, u32[]{:S(2)}, u32[]{:S(2)}) async-start(bf16[2048,5,128]{2,1,0:T(8,128)(2,1)} %copy.31), calls=%async_computation.3 | async-start | bytes 8388608 | tf_op jit(solution)/shard_map/all_to_all | solution.py:39
  438.2 332.4 %all-to-all-start.1 = ((f32[2048,5,128]{2,1,0:T(8,128)}), f32[2048,5,128]{2,1,0:T(8,128)}, u32[]{:S(2)}, u32[]{:S(2)}) async-start(f32[2048,5,128]{2,1,0:T(8,128)} %copy.27), calls=%async_computation.1 | async-start | bytes 16777216 | tf_op jit(solution)/shard_map/all_to_all | solution.py:29
  457.5 455.6 %all-reduce.2.cloned.1.call-start = ((), (), s32[]{:S(2)}) async-start(), calls=%async_computation.4 | async-start | bytes 33554432 | tf_op jit(solution)/shard_map/psum | solution.py:35
Sparse Core Ops, SparseCore 0:
  469.8 443.1 all-reduce.1
where the time goes:
time: 933 us; the launch traced here: 932 us
  waiting for transfers between devices  336 us (36%)
  blocking collectives  272 us (29%)
  local copies, waits for them, and re-layouts  151 us (16%)
  matrix products  82.9 us (9%)
  starting transfers between devices  67.3 us (7%)
  between operations  14.1 us (2%)
    psum x1, blocking collectives, local(): grad_weight, grad_bias = lax.psum((weight_part, bias_part), ('feat', 'rep'))  272 us
    psum x1, waiting for transfers between devices, local(): grad_weight, grad_bias = lax.psum((weight_part, bias_part), ('feat', 'rep'))  127 us
    all_to_all x1, waiting for transfers between devices, local(): lax.all_to_all(agg_low, 'feat', split_axis=2, concat_axis=0, tiled=True)  75.1 us
    all_to_all x1, waiting for transfers between devices, local(): lax.all_to_all(cotangent, 'feat', split_axis=2, concat_axis=0, tiled=True)  71.2 us
    all_to_all x1, waiting for transfers between devices, local(): lax.all_to_all(grad_rows, 'feat', split_axis=0, concat_axis=2, tiled=True)  63.4 us
    unnamed x11, local copies, waits for them, and re-layouts  61.7 us
    gather x1, local copies, waits for them, and re-layouts, local(): diagonal = jnp.diagonal(adjacency, axis1=1, axis2=2).astype(jnp.float32)  24.4 us
    dot_general x1, matrix products, local(): jnp.einsum('fg,fcr->gcr', weight, agg_rows, preferred_element_type=jnp.fl...  21.6 us
  transfers between devices with their start and end apart: 5, of which 4 were waited for; matrix products, arithmetic and copies ran while one was open for 7% of the time, Pallas kernels for 0%

commit v1 on v0

v1 whole, which is shorter than its diff:
```python
import functools

import jax
import jax.numpy as jnp
from jax import lax
from jax.experimental import pallas as pl
from jax.experimental.pallas import tpu as pltpu
from jax.sharding import PartitionSpec as P

TILE = 128
ROWS = 512
F32 = jnp.float32
BF16 = jnp.bfloat16
BUCKETS = (40, 48, 56, 64, 72, 80)


def params(mib=48):
    return pltpu.CompilerParams(vmem_limit_bytes=mib * 1024 * 1024)


def cost(flops, moved, transcendentals=0):
    return pl.CostEstimate(flops=flops, bytes_accessed=moved, transcendentals=transcendentals)


def dot(a, b, ca, cb):
    return lax.dot_general(a, b, (((ca,), (cb,)), ((), ())), preferred_element_type=F32)


def eye():
    row = lax.broadcasted_iota(jnp.int32, (TILE, TILE), 0)
    return row == lax.broadcasted_iota(jnp.int32, (TILE, TILE), 1)


def aligned(index, size=TILE):
    return pl.ds(pl.multiple_of(index * TILE, TILE), size)


def clear_tail(out_ref, first, last):
    def body(p, carry):
        out_ref[aligned(p), :] = jnp.zeros((TILE, out_ref.shape[1]), out_ref.dtype)
        return carry

    lax.fori_loop(first, last, body, 0)


def pack_kernel(clusters, counts, offsets, in_ref, out_ref):
    features = in_ref.shape[1]
    for c in range(clusters):
        live = counts[c]
        start = offsets[c]

        def body(t, carry):
            lane = t * TILE + lax.broadcasted_iota(jnp.int32, (features, TILE), 1)
            block = jnp.where(lane < live, in_ref[c, :, aligned(t)].astype(F32), 0.0)
            out_ref[aligned(start + t), :] = block.T.astype(out_ref.dtype)
            return carry

        lax.fori_loop(0, offsets[c + 1] - start, body, 0)
    clear_tail(out_ref, offsets[clusters], out_ref.shape[0] // TILE)


def pack(tiles, counts, offsets, values):
    clusters, features, nodes = values.shape
    size = tiles * TILE * features
    return pl.pallas_call(
        functools.partial(pack_kernel, clusters),
        out_shape=jax.ShapeDtypeStruct((tiles * TILE, features), BF16),
        grid_spec=pltpu.PrefetchScalarGridSpec(
            num_scalar_prefetch=2,
            grid=(1,),
            in_specs=[pl.BlockSpec((clusters, features, nodes), lambda i, *_: (0, 0, 0))],
            out_specs=pl.BlockSpec((tiles * TILE, features), lambda i, *_: (0, 0)),
        ),
        compiler_params=params(),
        cost_estimate=cost(size, 4 * size),
    )(counts, offsets, values)


def unpack_kernel(counts, offsets, in_ref, out_ref):
    c = pl.program_id(0)
    features = out_ref.shape[1]
    live = counts[c]
    start = offsets[c]

    def body(t, carry):
        lane = t * TILE + lax.broadcasted_iota(jnp.int32, (features, TILE), 1)
        block = in_ref[aligned(start + t), :].astype(F32).T
        out_ref[0, :, aligned(t)] = jnp.where(lane < live, block, 0.0)
        return carry

    def clear(t, carry):
        out_ref[0, :, aligned(t)] = jnp.zeros((features, TILE), F32)
        return carry

    used = offsets[c + 1] - start
    lax.fori_loop(0, used, body, 0)
    lax.fori_loop(used, out_ref.shape[2] // TILE, clear, 0)


def unpack(shape, counts, offsets, packed):
    clusters, features, nodes = shape
    return pl.pallas_call(
        unpack_kernel,
        out_shape=jax.ShapeDtypeStruct(shape, F32),
        grid_spec=pltpu.PrefetchScalarGridSpec(
            num_scalar_prefetch=2,
            grid=(clusters,),
            in_specs=[pl.BlockSpec(packed.shape, lambda c, *_: (0, 0))],
            out_specs=pl.BlockSpec((1, features, nodes), lambda c, *_: (c, 0, 0)),
        ),
        compiler_params=params(),
        cost_estimate=cost(packed.size, 2 * packed.size + 4 * clusters * features * nodes),
    )(counts, offsets, packed)


def adjacency_spec(nodes):
    def index(c, i, counts, offsets):
        return (c, jnp.minimum(i, (counts[c] - 1) // ROWS), 0)

    return pl.BlockSpec((1, ROWS, nodes), index)


def aggregate_kernel(clusters, counts, offsets, x_ref, a_ref, out_ref, masked):
    c = pl.program_id(0)
    i = pl.program_id(1)
    live = counts[c]

    @pl.when(jnp.logical_and(c == 0, i == 0))
    def _():
        clear_tail(out_ref, offsets[clusters], out_ref.shape[0] // TILE)

    @pl.when(i == 0)
    def _():
        lane = lax.broadcasted_iota(jnp.int32, masked.shape, 1)
        masked[...] = jnp.where(lane < live, x_ref[0].astype(F32), 0.0).astype(BF16)

    @pl.when(i * ROWS < live)
    def _():
        total = dot(a_ref[0], masked[...], 1, 1)
        for s in range(ROWS // TILE):
            t = i * (ROWS // TILE) + s

            @pl.when(t * TILE < live)
            def _():
                block = a_ref[0, s * TILE : (s + 1) * TILE, aligned(t)]
                block = jnp.where(eye(), block.astype(F32), 0.0).astype(BF16)
                extra = dot(block, masked[:, aligned(t)], 1, 1)
                rows = total[s * TILE : (s + 1) * TILE] + extra
                out_ref[aligned(offsets[c] + t), :] = rows.astype(BF16)


def aggregate(tiles, counts, offsets, features, adjacency):
    clusters, width, nodes = features.shape
    return pl.pallas_call(
        functools.partial(aggregate_kernel, clusters),
        out_shape=jax.ShapeDtypeStruct((tiles * TILE, width), BF16),
        grid_spec=pltpu.PrefetchScalarGridSpec(
            num_scalar_prefetch=2,
            grid=(clusters, nodes // ROWS),
            in_specs=[
                pl.BlockSpec((1, width, nodes), lambda c, i, *_: (c, 0, 0)),
                adjacency_spec(nodes),
            ],
            out_specs=pl.BlockSpec((tiles * TILE, width), lambda c, i, *_: (0, 0)),
            scratch_shapes=[pltpu.VMEM((width, nodes), BF16)],
        ),
        compiler_params=params(),
        cost_estimate=cost(2 * adjacency.size * width, 2 * adjacency.size),
    )(counts, offsets, features, adjacency)


def spread_kernel(counts, offsets, g_ref, a_ref, out_ref, turned):
    c = pl.program_id(0)
    i = pl.program_id(1)
    live = counts[c]
    width = out_ref.shape[1]

    @pl.when(i == 0)
    def _():
        out_ref[...] = jnp.zeros_like(out_ref)

    @pl.when(i * ROWS < live)
    def _():
        for s in range(ROWS // TILE):
            t = i * (ROWS // TILE) + s
            place = jnp.minimum(offsets[c] + t, g_ref.shape[0] // TILE - 1)
            lane = t * TILE + lax.broadcasted_iota(jnp.int32, (width, TILE), 1)
            block = g_ref[aligned(place), :].astype(F32).T
            turned[:, s * TILE : (s + 1) * TILE] = jnp.where(lane < live, block, 0.0).astype(BF16)
        out_ref[0] += dot(turned[...], a_ref[0], 1, 0)
        for s in range(ROWS // TILE):
            t = i * (ROWS // TILE) + s
            block = a_ref[0, s * TILE : (s + 1) * TILE, aligned(t)]
            block = jnp.where(eye(), block.astype(F32), 0.0).astype(BF16)
            extra = dot(turned[:, s * TILE : (s + 1) * TILE], block, 1, 0)
            out_ref[0, :, aligned(t)] += extra

    @pl.when(i == pl.num_programs(1) - 1)
    def _():
        lane = lax.broadcasted_iota(jnp.int32, out_ref.shape[1:], 1)
        out_ref[0] = jnp.where(lane < live, out_ref[0], 0.0)


def spread(counts, offsets, packed, adjacency):
    clusters, nodes, _ = adjacency.shape
    width = packed.shape[1]
    return pl.pallas_call(
        spread_kernel,
        out_shape=jax.ShapeDtypeStruct((clusters, width, nodes), F32),
        grid_spec=pltpu.PrefetchScalarGridSpec(
            num_scalar_prefetch=2,
            grid=(clusters, nodes // ROWS),
            in_specs=[
                pl.BlockSpec(packed.shape, lambda c, i, *_: (0, 0)),
                adjacency_spec(nodes),
            ],
            out_specs=pl.BlockSpec((1, width, nodes), lambda c, i, *_: (c, 0, 0)),
            scratch_shapes=[pltpu.VMEM((width, ROWS), BF16)],
        ),
        compiler_params=params(),
        cost_estimate=cost(2 * adjacency.size * width, 2 * adjacency.size),
    )(counts, offsets, packed, adjacency)


def middle_kernel(agg_ref, cot_ref, w_ref, b_ref, act_ref, low_ref, bias_ref, held):
    owners, _, width = agg_ref.shape

    @pl.when(pl.program_id(0) == 0)
    def _():
        for s in range(owners):
            held[:, s * width : (s + 1) * width] = agg_ref[s]

    pre = dot(held[...], w_ref[...], 1, 0) + b_ref[...].astype(F32)
    parts = cot_ref.shape[0]
    cot = jnp.concatenate([cot_ref[k] for k in range(parts)], axis=1).astype(F32)
    cdf = 0.5 + 0.5 * lax.erf(pre * (0.5**0.5))
    pdf = jnp.exp(-0.5 * pre * pre) * 0.3989422804014327
    act = (pre * cdf).astype(BF16)
    grad = cot * (cdf + pre * pdf)
    for k in range(parts):
        act_ref[k] = act[:, k * width : (k + 1) * width]
    low_ref[...] = grad.astype(BF16)
    bias_ref[...] = jnp.sum(grad, axis=0, keepdims=True)


def middle(agg, cot, weight, bias):
    owners, rows, width = agg.shape
    full = owners * width
    block = 256
    return pl.pallas_call(
        middle_kernel,
        out_shape=(
            jax.ShapeDtypeStruct((owners, rows, width), BF16),
            jax.ShapeDtypeStruct((rows, full), BF16),
            jax.ShapeDtypeStruct((1, full), F32),
        ),
        grid=(full // block,),
        in_specs=[
            pl.BlockSpec((owners, rows, width), lambda g: (0, 0, 0)),
            pl.BlockSpec((block // width, rows, width), lambda g: (g, 0, 0)),
            pl.BlockSpec((full, block), lambda g: (0, g)),
            pl.BlockSpec((1, block), lambda g: (0, g)),
        ],
        out_specs=(
            pl.BlockSpec((block // width, rows, width), lambda g: (g, 0, 0)),
            pl.BlockSpec((rows, block), lambda g: (0, g)),
            pl.BlockSpec((1, block), lambda g: (0, g)),
        ),
        scratch_shapes=[pltpu.VMEM((rows, full), BF16)],
        compiler_params=params(),
        cost_estimate=cost(2 * rows * full * full, 2 * full * full + 8 * rows * full, 2 * rows * full),
    )(agg, cot, weight, bias[None])


def outer_kernel(which, agg_ref, low_ref, out_ref):
    left = jnp.concatenate([agg_ref[s] for s in range(agg_ref.shape[0])], axis=1)
    out_ref[...] = dot(left, low_ref[...], 0, 0).astype(out_ref.dtype)


def outer(which, count, agg, low, dtype):
    owners, rows, width = agg.shape
    full = owners * width
    part = full // count
    step = min(part, 256)
    steps = part // step
    return pl.pallas_call(
        outer_kernel,
        out_shape=jax.ShapeDtypeStruct((part, full), dtype),
        grid_spec=pltpu.PrefetchScalarGridSpec(
            num_scalar_prefetch=1,
            grid=(steps,),
            in_specs=[
                pl.BlockSpec((step // width, rows, width), lambda i, which: (which[0] * steps + i, 0, 0)),
                pl.BlockSpec((rows, full), lambda i, which: (0, 0)),
            ],
            out_specs=pl.BlockSpec((step, full), lambda i, which: (i, 0)),
        ),
        compiler_params=params(),
        cost_estimate=cost(2 * rows * part * full, 4 * rows * full + 4 * part * full),
    )(which[None], agg, low)


def back_kernel(low_ref, w_ref, out_ref):
    width = out_ref.shape[2]
    value = dot(low_ref[...], w_ref[...], 1, 1).astype(BF16)
    for s in range(out_ref.shape[0]):
        out_ref[s] = value[:, s * width : (s + 1) * width]


def back(low, weight, owners):
    rows, full = low.shape
    width = full // owners
    step = 256
    return pl.pallas_call(
        back_kernel,
        out_shape=jax.ShapeDtypeStruct((owners, rows, width), BF16),
        grid=(full // step,),
        in_specs=[
            pl.BlockSpec((rows, full), lambda i: (0, 0)),
            pl.BlockSpec((step, full), lambda i: (i, 0)),
        ],
        out_specs=pl.BlockSpec((step // width, rows, width), lambda i: (i, 0, 0)),
        compiler_params=params(),
        cost_estimate=cost(2 * rows * full * full, 2 * full * full + 4 * rows * full),
    )(low, weight)


def swap_feat(value, bit):
    count = lax.axis_size("feat")
    return lax.ppermute(value, "feat", [(i, i ^ (1 << bit)) for i in range(count)])


def swap_rep(value):
    return lax.ppermute(value, "rep", [(0, 1), (1, 0)])


def joined(mine, own, other):
    first = mine == 0
    return jnp.concatenate([jnp.where(first, own, other), jnp.where(first, other, own)], axis=0)


def exchange(packed):
    owners = lax.axis_size("feat")
    blocks = packed.reshape(owners, -1, packed.shape[-1])
    return lax.all_to_all(blocks, "feat", split_axis=0, concat_axis=0, tiled=True)


def weight_sum(agg, low, bias_part):
    me = lax.axis_index("feat")
    core = lax.axis_index("rep")
    bits = lax.axis_size("feat").bit_length() - 1
    orders = [list(range(bits)), [1, 0] + list(range(2, bits))]
    chunks = len(orders)
    bias_part = bias_part + swap_rep(bias_part)
    sent = [
        swap_rep(outer((1 - core) * chunks + k, 2 * chunks, agg, low, BF16)) for k in range(chunks)
    ]
    sums = [
        outer(core * chunks + k, 2 * chunks, agg, low, F32) + sent[k].astype(F32)
        for k in range(chunks)
    ]
    for stage in range(bits):
        bias_part = bias_part + swap_feat(bias_part, stage)
        for k in range(chunks):
            bit = orders[k][stage]
            mine = (me >> bit) & 1
            half = sums[k].shape[0] // 2
            away = lax.dynamic_slice_in_dim(sums[k], (1 - mine) * half, half, 0).astype(BF16)
            kept = lax.dynamic_slice_in_dim(sums[k], mine * half, half, 0)
            sums[k] = kept + swap_feat(away, bit).astype(F32)
    owned = [value.astype(BF16) for value in sums]
    for stage in reversed(range(bits)):
        for k in range(chunks):
            bit = orders[k][stage]
            owned[k] = joined((me >> bit) & 1, owned[k], swap_feat(owned[k], bit))
    other = [swap_rep(value) for value in owned]
    own = jnp.concatenate(owned, axis=0)
    other = jnp.concatenate(other, axis=0)
    return joined(core, own, other).astype(F32), bias_part[0]


def run(tiles, features, adjacency, counts, offsets, weight, bias, cotangent):
    owners = lax.axis_size("feat")
    cot = exchange(pack(tiles, counts, offsets, cotangent))
    agg = exchange(aggregate(tiles, counts, offsets, features, adjacency))
    act, low, bias_part = middle(agg, cot, weight, bias)
    act = exchange(act).reshape(tiles * TILE, -1)
    grad_rows = exchange(back(low, weight, owners)).reshape(tiles * TILE, -1)
    grad_weight, grad_bias = weight_sum(agg, low, bias_part)
    activations = unpack(features.shape, counts, offsets, act)
    grad_features = spread(counts, offsets, grad_rows, adjacency)
    return activations, grad_features, grad_weight, grad_bias


def local(features, adjacency, counts, weight, bias, cotangent):
    features = features.transpose(1, 0, 2)
    cotangent = cotangent.transpose(1, 0, 2)
    clusters, _, nodes = features.shape
    used = (counts + TILE - 1) // TILE
    before = jnp.arange(clusters)[None] < jnp.arange(clusters + 1)[:, None]
    offsets = jnp.sum(jnp.where(before, used[None], 0), axis=1).astype(jnp.int32)
    need = offsets[-1:]
    need = jnp.maximum(need, swap_rep(need))[0]
    most = clusters * nodes // TILE
    buckets = [b for b in BUCKETS if b < most] + [most]
    branch = sum([(need > b).astype(jnp.int32) for b in buckets[:-1]], jnp.int32(0))
    branches = [functools.partial(run, b) for b in buckets]
    args = (features, adjacency, counts, offsets, weight, bias, cotangent)
    activations, grad_features, grad_weight, grad_bias = lax.switch(branch, branches, *args)
    return (
        activations.transpose(1, 0, 2),
        grad_features.transpose(1, 0, 2),
        grad_weight,
        grad_bias,
    )


def solution(mesh):
    placed = (
        P("feat", "rep", None),
        P("rep", None, None),
        P("rep"),
        P(),
        P(),
        P("feat", "rep", None),
    )
    return jax.shard_map(
        local,
        mesh=mesh,
        in_specs=placed,
        out_specs=(P("feat", "rep", None), P("feat", "rep", None), P(), P()),
        check_vma=False,
    )
```

time: 933 us -> 453 us (0.49)
  blocking collectives: 272 us -> 0 us
  local copies, waits for them, and re-layouts: 151 us -> 18.8 us
  waiting for transfers between devices: 336 us -> 206 us
  Pallas kernels: 0 us -> 99.9 us
  matrix products: 82.9 us -> 0 us
  other arithmetic: 7.92 us -> 36.4 us
  loops' own time: 0 us -> 15.2 us
  between operations: 14.1 us -> 2.71 us
    psum x1 -> x0, blocking collectives: 272 us -> none  [local(): grad_weight, grad_bias = lax.psum((weight_part, bias_part), ('feat', 'rep'))]
    all_to_all x4, waiting for transfers between devices: 210 us -> 73.5 us  [exchange(): lax.all_to_all(blocks, 'feat', split_axis=0, concat_axis=0, tiled=True)]
    ppermute x0 -> x26, waiting for transfers between devices: none -> 133 us  [the longest x20 129 us: swap_feat(): lax.ppermute(value, 'feat', [(i, i ^ 1 << bit) for i in range(count)])]
    psum x1 -> x0, waiting for transfers between devices: 127 us -> none  [local(): grad_weight, grad_bias = lax.psum((weight_part, bias_part), ('feat', 'rep'))]
    pallas_call x0 -> x10, Pallas kernels: none -> 99.9 us  [the longest x1 27.3 us: aggregate(): pl.pallas_call(functools.partial(aggregate_kernel, clusters), out_shape=j...]
    dot_general x5 -> x0, matrix products: 82.9 us -> none  [the longest x1 21.6 us: local(): jnp.einsum('fg,fcr->gcr', weight, agg_rows, preferred_element_type=jnp.fl...]
    unnamed x11 -> x57, local copies, waits for them, and re-layouts: 61.7 us -> 14.9 us
    all_to_all x4, starting transfers between devices: 67.3 us -> 31.1 us  [exchange(): lax.all_to_all(blocks, 'feat', split_axis=0, concat_axis=0, tiled=True)]
  transfers between devices with their start and end apart: 5 -> 30, of which waited for: 4 -> 21; matrix products, arithmetic and copies ran while one was open for 7% -> 5% of each run, Pallas kernels for 0% -> 13%
where the time goes in v1:
time: 453 us; the launch traced here: 446 us
  waiting for transfers between devices  206 us (45%)
  Pallas kernels  99.9 us (22%)
  starting transfers between devices  66.5 us (15%)
  other arithmetic  36.4 us (8%)
  local copies, waits for them, and re-layouts  18.8 us (4%)
  loops' own time  15.2 us (3%)
    ppermute x20, waiting for transfers between devices, swap_feat(): lax.ppermute(value, 'feat', [(i, i ^ 1 << bit) for i in range(count)])  129 us
    all_to_all x4, waiting for transfers between devices, exchange(): lax.all_to_all(blocks, 'feat', split_axis=0, concat_axis=0, tiled=True)  73.5 us
    ppermute x20, starting transfers between devices, swap_feat(): lax.ppermute(value, 'feat', [(i, i ^ 1 << bit) for i in range(count)])  33.9 us
    all_to_all x4, starting transfers between devices, exchange(): lax.all_to_all(blocks, 'feat', split_axis=0, concat_axis=0, tiled=True)  31.1 us
    pallas_call x1, Pallas kernels, aggregate(): pl.pallas_call(functools.partial(aggregate_kernel, clusters), out_shape=j...  27.3 us
    pallas_call x1, Pallas kernels, spread(): pl.pallas_call(spread_kernel, out_shape=jax.ShapeDtypeStruct((clusters, w...  24.5 us
    unnamed x1, loops' own time  15.2 us
    unnamed x57, local copies, waits for them, and re-layouts  14.9 us
  transfers between devices with their start and end apart: 30, of which 21 were waited for; matrix products, arithmetic and copies ran while one was open for 5% of the time, Pallas kernels for 13%

profile of v1, /device:TPU:0, one launch (start us, length us, event | category | flops | bytes accessed | tf_op | source)
XLA Modules:
  0.0 445.8 jit_solution(3128013106555619656)
XLA Ops:
  4.7 439.7 %conditional.4 = (f32[5,128,2048]{2,1,0:T(8,128)}, f32[5,128,2048]{2,1,0:T(8,128)}, f32[2048]{0:T(1024)S(1)}, f32[2048,2048]{1,0:T(8,128)}) conditional(s32[]{:T(128)} %bitcast.54, (s32[5]{0:T(128)}, s32[6]{0:T(128)S(1)}, bf16[5,128,2048]{2,1,0:T(8,128)(2,1)}, bf16[5,2048,2048]{2,1,0:T(8,128)(2,1)}, ...), branch_computations={%region_1.2_spmd, %region_2.3_spmd, %region_3.4_spmd, %region_4.5_... | conditional | flops 26919184384 | bytes 621594368
  12.8 27.3 %branch_3_fun.10 = bf16[8192,128]{1,0:T(8,128)(2,1)S(1)} custom-call(s32[5]{0:T(128)} %get-tuple-element.126.counts, s32[6]{0:T(128)S(1)} %get-tuple-element.127.offsets, bf16[5,128,2048]{2,1,0:T(8,128)(2,1)} %get-tuple-element.128.x_ref, bf16[5,2048,2048]{2,1,0:T(8,128)(2,1)} %get-tuple-element.129.a_ref), custom_call_target="tpu_custom_call" | custom-call | flops 5368709120 | bytes 41943040 | tf_op jit(solution)/shard_map/cond/branch_3_fun/pallas_call | solution.py:154
  41.4 8.3 %all-to-all-start.12 = ((bf16[16,512,128]{2,1,0:T(8,128)(2,1)}), bf16[16,512,128]{2,1,0:T(8,128)(2,1)S(1)}, u32[]{:S(2)}, u32[]{:S(2)}) async-start(bf16[16,512,128]{2,1,0:T(8,128)(2,1)} %bitcast.65), calls=%async_computation.12 | async-start | bytes 4194304 | tf_op jit(solution)/shard_map/cond/branch_3_fun/all_to_all | solution.py:345
  49.7 8.5 %branch_3_fun.11 = bf16[8192,128]{1,0:T(8,128)(2,1)S(1)} custom-call(s32[5]{0:T(128)S(1)} %copy-done.139, s32[6]{0:T(128)S(1)} %get-tuple-element.127.offsets, bf16[5,128,2048]{2,1,0:T(8,128)(2,1)} %get-tuple-element.130.in_ref), custom_call_target="tpu_custom_call" | custom-call | flops 1048576 | bytes 4194304 | tf_op jit(solution)/shard_map/cond/branch_3_fun/pallas_call | solution.py:65
  59.6 31.1 %all-to-all-done.12.agg_ref = bf16[16,512,128]{2,1,0:T(8,128)(2,1)S(1)} async-done(((bf16[16,512,128]{2,1,0:T(8,128)(2,1)}), bf16[16,512,128]{2,1,0:T(8,128)(2,1)S(1)}, u32[]{:S(2)}, u32[]{:S(2)}) %all-to-all-start.12) | async-done | bytes 2097184 | tf_op jit(solution)/shard_map/cond/branch_3_fun/all_to_all | solution.py:345
  90.6 9.7 %all-to-all-start.13 = ((bf16[16,512,128]{2,1,0:T(8,128)(2,1)}), bf16[16,512,128]{2,1,0:T(8,128)(2,1)}, u32[]{:S(2)}, u32[]{:S(2)}) async-start(bf16[16,512,128]{2,1,0:T(8,128)(2,1)} %bitcast.66), calls=%async_computation.13 | async-start | bytes 4194304 | tf_op jit(solution)/shard_map/cond/branch_3_fun/all_to_all | solution.py:345
  100.4 42.4 %all-to-all-done.13.cot_ref = bf16[16,512,128]{2,1,0:T(8,128)(2,1)} async-done(((bf16[16,512,128]{2,1,0:T(8,128)(2,1)}), bf16[16,512,128]{2,1,0:T(8,128)(2,1)}, u32[]{:S(2)}, u32[]{:S(2)}) %all-to-all-start.13) | async-done | bytes 2097184 | tf_op jit(solution)/shard_map/cond/branch_3_fun/all_to_all | solution.py:345
  142.9 11.5 %branch_3_fun.12 = (bf16[16,512,128]{2,1,0:T(8,128)(2,1)S(1)}, bf16[512,2048]{1,0:T(8,128)(2,1)S(1)}, f32[1,2048]{1,0:T(1,128)S(1)}) custom-call(bf16[16,512,128]{2,1,0:T(8,128)(2,1)} %copy-done.6, bf16[16,512,128]{2,1,0:T(8,128)(2,1)} %all-to-all-done.13.cot_ref, bf16[2048,2048]{1,0:T(8,128)(2,1)} %get-tuple-element.131.w_ref, ...), custom_call_target="tpu_custom_call" | custom-call | flops 4294967296 | bytes 16777216 | tf_op jit(solution)/shard_map/cond/branch_3_fun/pallas_call | solution.py:250
  158.7 4.2 branch_3_fun.17
  162.9 4.1 branch_3_fun.19
  174.6 3.6 convert_add_fusion.25
  185.2 3.4 collective-permute-start.90
  188.6 7.6 %all-to-all-start.14 = ((bf16[16,512,128]{2,1,0:T(8,128)(2,1)}), bf16[16,512,128]{2,1,0:T(8,128)(2,1)S(1)}, u32[]{:S(2)}, u32[]{:S(2)}) async-start(bf16[16,512,128]{2,1,0:T(8,128)(2,1)} %copy-done.36), calls=%async_computation.14 | async-start | bytes 4194304 | tf_op jit(solution)/shard_map/cond/branch_3_fun/all_to_all | solution.py:345
  196.3 9.6 %collective-permute-done.81 = bf16[256,2048]{1,0:T(8,128)(2,1)} collective-permute-done((bf16[256,2048]{1,0:T(8,128)(2,1)}, bf16[256,2048]{1,0:T(8,128)(2,1)}, u32[]{:S(2)}, u32[]{:S(2)}) %collective-permute-start.81) | collective-permute-done | bytes 1048608 | tf_op jit(solution)/shard_map/cond/branch_3_fun/ppermute | solution.py:330
  211.6 17.5 %collective-permute-done.90 = bf16[256,2048]{1,0:T(8,128)(2,1)} collective-permute-done((bf16[256,2048]{1,0:T(8,128)(2,1)S(1)}, bf16[256,2048]{1,0:T(8,128)(2,1)}, u32[]{:S(2)}, u32[]{:S(2)}) %collective-permute-start.90) | collective-permute-done | bytes 1048608 | tf_op jit(solution)/shard_map/cond/branch_3_fun/ppermute | solution.py:330
  231.7 14.0 %collective-permute-done.82 = bf16[128,2048]{1,0:T(8,128)(2,1)S(1)} collective-permute-done((bf16[128,2048]{1,0:T(8,128)(2,1)S(1)}, bf16[128,2048]{1,0:T(8,128)(2,1)S(1)}, u32[]{:S(2)}, u32[]{:S(2)}) %collective-permute-start.82) | collective-permute-done | bytes 524320 | tf_op jit(solution)/shard_map/cond/branch_3_fun/ppermute | solution.py:330
  245.9 5.2 %collective-permute-start.83 = (bf16[64,2048]{1,0:T(8,128)(2,1)S(1)}, bf16[64,2048]{1,0:T(8,128)(2,1)S(1)}, u32[]{:S(2)}, u32[]{:S(2)}) collective-permute-start(bf16[64,2048]{1,0:T(8,128)(2,1)S(1)} %dynamic-slice_convert_fusion.29), channel_id=1, source_target_pairs={{0,8},{2,10},{4,12},{6,14},{8,0},{10,2},{12,4},{14,6},{16,24},{18,... | collective-permute-start | bytes 786440 | tf_op jit(solution)/shard_map/cond/branch_3_fun/ppermute | solution.py:330
  253.3 4.9 %collective-permute-done.83 = bf16[64,2048]{1,0:T(8,128)(2,1)S(1)} collective-permute-done((bf16[64,2048]{1,0:T(8,128)(2,1)S(1)}, bf16[64,2048]{1,0:T(8,128)(2,1)S(1)}, u32[]{:S(2)}, u32[]{:S(2)}) %collective-permute-start.83) | collective-permute-done | bytes 262176 | tf_op jit(solution)/shard_map/cond/branch_3_fun/ppermute | solution.py:330
  261.2 4.2 collective-permute-done.92
  269.4 6.0 %collective-permute-done.93 = bf16[32,2048]{1,0:T(8,128)(2,1)S(1)} collective-permute-done((bf16[32,2048]{1,0:T(8,128)(2,1)S(1)}, bf16[32,2048]{1,0:T(8,128)(2,1)S(1)}, u32[]{:S(2)}, u32[]{:S(2)}) %collective-permute-start.93) | collective-permute-done | bytes 131104 | tf_op jit(solution)/shard_map/cond/branch_3_fun/ppermute | solution.py:330
  278.7 5.2 %collective-permute-done.94 = bf16[32,2048]{1,0:T(8,128)(2,1)S(1)} collective-permute-done((bf16[32,2048]{1,0:T(8,128)(2,1)S(1)}, bf16[32,2048]{1,0:T(8,128)(2,1)S(1)}, u32[]{:S(2)}, u32[]{:S(2)}) %collective-permute-start.94) | collective-permute-done | bytes 131104 | tf_op jit(solution)/shard_map/cond/branch_3_fun/ppermute | solution.py:330
  284.0 5.5 %collective-permute-done.86 = bf16[64,2048]{1,0:T(8,128)(2,1)S(1)} collective-permute-done((bf16[64,2048]{1,0:T(8,128)(2,1)S(1)}, bf16[64,2048]{1,0:T(8,128)(2,1)S(1)}, u32[]{:S(2)}, u32[]{:S(2)}) %collective-permute-start.86) | collective-permute-done | bytes 262176 | tf_op jit(solution)/shard_map/cond/branch_3_fun/ppermute | solution.py:330
  291.4 3.5 collective-permute-done.95
  297.0 6.2 %collective-permute-done.87 = bf16[128,2048]{1,0:T(8,128)(2,1)S(1)} collective-permute-done((bf16[128,2048]{1,0:T(8,128)(2,1)S(1)}, bf16[128,2048]{1,0:T(8,128)(2,1)S(1)}, u32[]{:S(2)}, u32[]{:S(2)}) %collective-permute-start.87) | collective-permute-done | bytes 524320 | tf_op jit(solution)/shard_map/cond/branch_3_fun/ppermute | solution.py:330
  304.7 6.0 %branch_3_fun.14 = bf16[16,512,128]{2,1,0:T(8,128)(2,1)S(1)} custom-call(bf16[512,2048]{1,0:T(8,128)(2,1)S(1)} %copy-done.15, bf16[2048,2048]{1,0:T(8,128)(2,1)S(1)} %bitcast.93), custom_call_target="tpu_custom_call" | custom-call | flops 4294967296 | bytes 12582912 | tf_op jit(solution)/shard_map/cond/branch_3_fun/pallas_call | solution.py:314
  312.1 5.5 %all-to-all-start.15 = ((bf16[16,512,128]{2,1,0:T(8,128)(2,1)}), bf16[16,512,128]{2,1,0:T(8,128)(2,1)}, u32[]{:S(2)}, u32[]{:S(2)}) async-start(bf16[16,512,128]{2,1,0:T(8,128)(2,1)} %copy-done.37), calls=%async_computation.15 | async-start | bytes 4194304 | tf_op jit(solution)/shard_map/cond/branch_3_fun/all_to_all | solution.py:345
  320.0 14.1 %collective-permute-done.88 = bf16[256,2048]{1,0:T(8,128)(2,1)} collective-permute-done((bf16[256,2048]{1,0:T(8,128)(2,1)}, bf16[256,2048]{1,0:T(8,128)(2,1)}, u32[]{:S(2)}, u32[]{:S(2)}) %collective-permute-start.88) | collective-permute-done | bytes 1048608 | tf_op jit(solution)/shard_map/cond/branch_3_fun/ppermute | solution.py:330
  337.6 25.3 %collective-permute-done.97 = bf16[256,2048]{1,0:T(8,128)(2,1)S(1)} collective-permute-done((bf16[256,2048]{1,0:T(8,128)(2,1)S(1)}, bf16[256,2048]{1,0:T(8,128)(2,1)S(1)}, u32[]{:S(2)}, u32[]{:S(2)}) %collective-permute-start.97) | collective-permute-done | bytes 1048608 | tf_op jit(solution)/shard_map/cond/branch_3_fun/ppermute | solution.py:330
  385.1 8.2 %branch_3_fun.13 = f32[5,128,2048]{2,1,0:T(8,128)} custom-call(s32[5]{0:T(128)S(1)} %copy-done.139, s32[6]{0:T(128)S(1)} %get-tuple-element.127.offsets, bf16[8192,128]{1,0:T(8,128)(2,1)S(1)} %bitcast.67), custom_call_target="tpu_custom_call" | custom-call | flops 1048576 | bytes 7340032 | tf_op jit(solution)/shard_map/cond/branch_3_fun/pallas_call | solution.py:102
  393.3 24.5 %branch_3_fun.15 = f32[5,128,2048]{2,1,0:T(8,128)} custom-call(s32[5]{0:T(128)S(1)} %copy-done.139, s32[6]{0:T(128)S(1)} %get-tuple-element.127.offsets, bf16[8192,128]{1,0:T(8,128)(2,1)} %bitcast.30.g_ref, bf16[5,2048,2048]{2,1,0:T(8,128)(2,1)} %get-tuple-element.129.a_ref), custom_call_target="tpu_custom_call" | custom-call | flops 5368709120 | bytes 41943040 | tf_op jit(solution)/shard_map/cond/branch_3_fun/pallas_call | solution.py:207
  421.5 4.6 %broadcast_select_fusion.55 = (bf16[1024,2048]{1,0:T(8,128)(2,1)}, bf16[1024,2048]{1,0:T(8,128)(2,1)}) fusion(bf16[1024,2048]{1,0:T(8,128)(2,1)S(1)} %constant_dynamic-update-slice_fusion.6, pred[]{:T(512)S(6)} %eq.90, bf16[256,2048]{1,0:T(8,128)(2,1)S(1)} %copy-done.100, bf16[256,2048]{1,0:T(8,128)(2,1)S(1)} %copy-done.98, ...), kind=kLoop, calls=%fused_computation.149 | loop fusion | flops 20971520 | bytes 16777216 | tf_op jit(solution)/shard_map/cond/branch_3_fun/jit(_where)/select_n | solution.py:339
  426.1 11.8 %maximum_convert_fusion.3 = f32[2048,2048]{1,0:T(8,128)} fusion(bf16[1024,2048]{1,0:T(8,128)(2,1)} %get-tuple-element.229, bf16[1024,2048]{1,0:T(8,128)(2,1)} %get-tuple-element.228), kind=kLoop, calls=%fused_computation.144 | loop fusion | flops 16777216 | bytes 25165824 | tf_op jit(solution)/shard_map/cond/branch_0_fun/convert_element_type | solution.py:379
  (143 shorter events, 84.5 us)
Async XLA Ops:
  2.0 1.4 collective-permute-start.150
  41.4 49.2 %all-to-all-start.12 = ((bf16[16,512,128]{2,1,0:T(8,128)(2,1)}), bf16[16,512,128]{2,1,0:T(8,128)(2,1)S(1)}, u32[]{:S(2)}, u32[]{:S(2)}) async-start(bf16[16,512,128]{2,1,0:T(8,128)(2,1)} %bitcast.65), calls=%async_computation.12 | async-start | bytes 4194304 | tf_op jit(solution)/shard_map/cond/branch_3_fun/all_to_all | solution.py:345
  90.6 52.2 %copy-start.6 = (bf16[16,512,128]{2,1,0:T(8,128)(2,1)}, bf16[16,512,128]{2,1,0:T(8,128)(2,1)S(1)}, u32[]{:S(2)}) copy-start(bf16[16,512,128]{2,1,0:T(8,128)(2,1)S(1)} %all-to-all-done.12.agg_ref) | copy-start | bytes 6291460
  90.6 52.2 %all-to-all-start.13 = ((bf16[16,512,128]{2,1,0:T(8,128)(2,1)}), bf16[16,512,128]{2,1,0:T(8,128)(2,1)}, u32[]{:S(2)}, u32[]{:S(2)}) async-start(bf16[16,512,128]{2,1,0:T(8,128)(2,1)} %bitcast.66), calls=%async_computation.13 | async-start | bytes 4194304 | tf_op jit(solution)/shard_map/cond/branch_3_fun/all_to_all | solution.py:345
  162.9 11.8 %collective-permute-start.80 = (bf16[512,2048]{1,0:T(8,128)(2,1)}, bf16[512,2048]{1,0:T(8,128)(2,1)}, u32[]{:S(2)}, u32[]{:S(2)}) collective-permute-start(bf16[512,2048]{1,0:T(8,128)(2,1)} %branch_3_fun.17), channel_id=1, source_target_pairs={{0,1},{1,0},{2,3},{3,2},{4,5},{5,4},{6,7},{7,6},{8,9},{9,8},{10,11... | collective-permute-start | bytes 6291464 | tf_op jit(solution)/shard_map/cond/branch_3_fun/ppermute | solution.py:334
  167.0 13.6 %collective-permute-start.89 = (bf16[512,2048]{1,0:T(8,128)(2,1)}, bf16[512,2048]{1,0:T(8,128)(2,1)}, u32[]{:S(2)}, u32[]{:S(2)}) collective-permute-start(bf16[512,2048]{1,0:T(8,128)(2,1)} %branch_3_fun.19), channel_id=1, source_target_pairs={{0,1},{1,0},{2,3},{3,2},{4,5},{5,4},{6,7},{7,6},{8,9},{9,8},{10,11... | collective-permute-start | bytes 6291464 | tf_op jit(solution)/shard_map/cond/branch_3_fun/ppermute | solution.py:334
  179.5 26.3 %collective-permute-start.81 = (bf16[256,2048]{1,0:T(8,128)(2,1)}, bf16[256,2048]{1,0:T(8,128)(2,1)}, u32[]{:S(2)}, u32[]{:S(2)}) collective-permute-start(bf16[256,2048]{1,0:T(8,128)(2,1)} %dynamic-slice_convert_fusion.25), channel_id=1, source_target_pairs={{0,2},{2,0},{4,6},{6,4},{8,10},{10,8},{12,14},{14,12},{16,18},{18,... | collective-permute-start | bytes 3145736 | tf_op jit(solution)/shard_map/cond/branch_3_fun/ppermute | solution.py:330
  185.2 43.8 %collective-permute-start.90 = (bf16[256,2048]{1,0:T(8,128)(2,1)S(1)}, bf16[256,2048]{1,0:T(8,128)(2,1)}, u32[]{:S(2)}, u32[]{:S(2)}) collective-permute-start(bf16[256,2048]{1,0:T(8,128)(2,1)S(1)} %dynamic-slice_convert_fusion.24), channel_id=1, source_target_pairs={{0,4},{2,6},{4,0},{6,2},{8,12},{10,14},{12,8},{14,10},{16,20},{18,... | collective-permute-start | bytes 3145736 | tf_op jit(solution)/shard_map/cond/branch_3_fun/ppermute | solution.py:330
  188.6 123.4 %all-to-all-start.14 = ((bf16[16,512,128]{2,1,0:T(8,128)(2,1)}), bf16[16,512,128]{2,1,0:T(8,128)(2,1)S(1)}, u32[]{:S(2)}, u32[]{:S(2)}) async-start(bf16[16,512,128]{2,1,0:T(8,128)(2,1)} %copy-done.36), calls=%async_computation.14 | async-start | bytes 4194304 | tf_op jit(solution)/shard_map/cond/branch_3_fun/all_to_all | solution.py:345
  208.2 37.5 %collective-permute-start.82 = (bf16[128,2048]{1,0:T(8,128)(2,1)S(1)}, bf16[128,2048]{1,0:T(8,128)(2,1)S(1)}, u32[]{:S(2)}, u32[]{:S(2)}) collective-permute-start(bf16[128,2048]{1,0:T(8,128)(2,1)S(1)} %dynamic-slice_convert_fusion.27), channel_id=1, source_target_pairs={{0,4},{2,6},{4,0},{6,2},{8,12},{10,14},{12,8},{14,10},{16,20},{18,... | collective-permute-start | bytes 1572872 | tf_op jit(solution)/shard_map/cond/branch_3_fun/ppermute | solution.py:330
  230.6 20.4 %collective-permute-start.91 = (bf16[128,2048]{1,0:T(8,128)(2,1)S(1)}, bf16[128,2048]{1,0:T(8,128)(2,1)S(1)}, u32[]{:S(2)}, u32[]{:S(2)}) collective-permute-start(bf16[128,2048]{1,0:T(8,128)(2,1)S(1)} %dynamic-slice_convert_fusion.26), channel_id=1, source_target_pairs={{0,2},{2,0},{4,6},{6,4},{8,10},{10,8},{12,14},{14,12},{16,18},{18,... | collective-permute-start | bytes 1572872 | tf_op jit(solution)/shard_map/cond/branch_3_fun/ppermute | solution.py:330
  245.7 59.0 %slice-start.4 = ((s8[8388608]{0:T(1024)(128)(4,1)}), s8[4194304]{0:T(1024)(128)(4,1)S(1)}, s32[]{:S(2)}) async-start(s8[8388608]{0:T(1024)(128)(4,1)} %bitcast.92), calls=%async_computation.28 | async-start | bytes 8388608
  245.9 12.4 %collective-permute-start.83 = (bf16[64,2048]{1,0:T(8,128)(2,1)S(1)}, bf16[64,2048]{1,0:T(8,128)(2,1)S(1)}, u32[]{:S(2)}, u32[]{:S(2)}) collective-permute-start(bf16[64,2048]{1,0:T(8,128)(2,1)S(1)} %dynamic-slice_convert_fusion.29), channel_id=1, source_target_pairs={{0,8},{2,10},{4,12},{6,14},{8,0},{10,2},{12,4},{14,6},{16,24},{18,... | collective-permute-start | bytes 786440 | tf_op jit(solution)/shard_map/cond/branch_3_fun/ppermute | solution.py:330
  251.2 14.2 %collective-permute-start.92 = (bf16[64,2048]{1,0:T(8,128)(2,1)S(1)}, bf16[64,2048]{1,0:T(8,128)(2,1)S(1)}, u32[]{:S(2)}, u32[]{:S(2)}) collective-permute-start(bf16[64,2048]{1,0:T(8,128)(2,1)S(1)} %dynamic-slice_convert_fusion.28), channel_id=1, source_target_pairs={{0,8},{2,10},{4,12},{6,14},{8,0},{10,2},{12,4},{14,6},{16,24},{18,... | collective-permute-start | bytes 786440 | tf_op jit(solution)/shard_map/cond/branch_3_fun/ppermute | solution.py:330
  258.3 7.9 %collective-permute-start.84 = (bf16[32,2048]{1,0:T(8,128)(2,1)S(1)}, bf16[32,2048]{1,0:T(8,128)(2,1)S(1)}, u32[]{:S(2)}, u32[]{:S(2)}) collective-permute-start(bf16[32,2048]{1,0:T(8,128)(2,1)S(1)} %dynamic-slice_convert_fusion.31), channel_id=1, source_target_pairs={{0,16},{2,18},{4,20},{6,22},{8,24},{10,26},{12,28},{14,30},{16,0},... | collective-permute-start | bytes 393224 | tf_op jit(solution)/shard_map/cond/branch_3_fun/ppermute | solution.py:330
  265.5 9.9 %collective-permute-start.93 = (bf16[32,2048]{1,0:T(8,128)(2,1)S(1)}, bf16[32,2048]{1,0:T(8,128)(2,1)S(1)}, u32[]{:S(2)}, u32[]{:S(2)}) collective-permute-start(bf16[32,2048]{1,0:T(8,128)(2,1)S(1)} %dynamic-slice_convert_fusion.30), channel_id=1, source_target_pairs={{0,16},{2,18},{4,20},{6,22},{8,24},{10,26},{12,28},{14,30},{16,0},... | collective-permute-start | bytes 393224 | tf_op jit(solution)/shard_map/cond/branch_3_fun/ppermute | solution.py:330
  266.3 11.9 %collective-permute-start.85 = (bf16[32,2048]{1,0:T(8,128)(2,1)S(1)}, bf16[32,2048]{1,0:T(8,128)(2,1)S(1)}, u32[]{:S(2)}, u32[]{:S(2)}) collective-permute-start(bf16[32,2048]{1,0:T(8,128)(2,1)S(1)} %add_convert_fusion.7), channel_id=1, source_target_pairs={{0,16},{2,18},{4,20},{6,22},{8,24},{10,26},{12,28},{14,30},{16,0},... | collective-permute-start | bytes 393224 | tf_op jit(solution)/shard_map/cond/branch_3_fun/ppermute | solution.py:330
  275.5 8.4 %collective-permute-start.94 = (bf16[32,2048]{1,0:T(8,128)(2,1)S(1)}, bf16[32,2048]{1,0:T(8,128)(2,1)S(1)}, u32[]{:S(2)}, u32[]{:S(2)}) collective-permute-start(bf16[32,2048]{1,0:T(8,128)(2,1)S(1)} %add_convert_fusion.6), channel_id=1, source_target_pairs={{0,16},{2,18},{4,20},{6,22},{8,24},{10,26},{12,28},{14,30},{16,0},... | collective-permute-start | bytes 393224 | tf_op jit(solution)/shard_map/cond/branch_3_fun/ppermute | solution.py:330
  278.2 11.3 %collective-permute-start.86 = (bf16[64,2048]{1,0:T(8,128)(2,1)S(1)}, bf16[64,2048]{1,0:T(8,128)(2,1)S(1)}, u32[]{:S(2)}, u32[]{:S(2)}) collective-permute-start(bf16[64,2048]{1,0:T(8,128)(2,1)S(1)} %pad_maximum_fusion.34), channel_id=1, source_target_pairs={{0,8},{2,10},{4,12},{6,14},{8,0},{10,2},{12,4},{14,6},{16,24},{18,... | collective-permute-start | bytes 786440 | tf_op jit(solution)/shard_map/cond/branch_3_fun/ppermute | solution.py:330
  284.0 10.9 %collective-permute-start.95 = (bf16[64,2048]{1,0:T(8,128)(2,1)S(1)}, bf16[64,2048]{1,0:T(8,128)(2,1)S(1)}, u32[]{:S(2)}, u32[]{:S(2)}) collective-permute-start(bf16[64,2048]{1,0:T(8,128)(2,1)S(1)} %pad_maximum_fusion.35), channel_id=1, source_target_pairs={{0,8},{2,10},{4,12},{6,14},{8,0},{10,2},{12,4},{14,6},{16,24},{18,... | collective-permute-start | bytes 786440 | tf_op jit(solution)/shard_map/cond/branch_3_fun/ppermute | solution.py:330
  289.7 13.5 %collective-permute-start.87 = (bf16[128,2048]{1,0:T(8,128)(2,1)S(1)}, bf16[128,2048]{1,0:T(8,128)(2,1)S(1)}, u32[]{:S(2)}, u32[]{:S(2)}) collective-permute-start(bf16[128,2048]{1,0:T(8,128)(2,1)S(1)} %pad_maximum_fusion.32), channel_id=1, source_target_pairs={{0,4},{2,6},{4,0},{6,2},{8,12},{10,14},{12,8},{14,10},{16,20},{18,... | collective-permute-start | bytes 1572872 | tf_op jit(solution)/shard_map/cond/branch_3_fun/ppermute | solution.py:330
  295.8 21.8 %collective-permute-start.96 = (bf16[128,2048]{1,0:T(8,128)(2,1)}, bf16[128,2048]{1,0:T(8,128)(2,1)S(1)}, u32[]{:S(2)}, u32[]{:S(2)}) collective-permute-start(bf16[128,2048]{1,0:T(8,128)(2,1)} %pad_maximum_fusion.33), channel_id=1, source_target_pairs={{0,2},{2,0},{4,6},{6,4},{8,10},{10,8},{12,14},{14,12},{16,18},{18,... | collective-permute-start | bytes 1572872 | tf_op jit(solution)/shard_map/cond/branch_3_fun/ppermute | solution.py:330
  304.6 29.6 %collective-permute-start.88 = (bf16[256,2048]{1,0:T(8,128)(2,1)}, bf16[256,2048]{1,0:T(8,128)(2,1)}, u32[]{:S(2)}, u32[]{:S(2)}) collective-permute-start(bf16[256,2048]{1,0:T(8,128)(2,1)} %pad_maximum_fusion.30), channel_id=1, source_target_pairs={{0,2},{2,0},{4,6},{6,4},{8,10},{10,8},{12,14},{14,12},{16,18},{18,... | collective-permute-start | bytes 3145736 | tf_op jit(solution)/shard_map/cond/branch_3_fun/ppermute | solution.py:330
  312.1 81.2 %all-to-all-start.15 = ((bf16[16,512,128]{2,1,0:T(8,128)(2,1)}), bf16[16,512,128]{2,1,0:T(8,128)(2,1)}, u32[]{:S(2)}, u32[]{:S(2)}) async-start(bf16[16,512,128]{2,1,0:T(8,128)(2,1)} %copy-done.37), calls=%async_computation.15 | async-start | bytes 4194304 | tf_op jit(solution)/shard_map/cond/branch_3_fun/all_to_all | solution.py:345
  317.9 45.0 %collective-permute-start.97 = (bf16[256,2048]{1,0:T(8,128)(2,1)S(1)}, bf16[256,2048]{1,0:T(8,128)(2,1)S(1)}, u32[]{:S(2)}, u32[]{:S(2)}) collective-permute-start(bf16[256,2048]{1,0:T(8,128)(2,1)S(1)} %pad_maximum_fusion.31), channel_id=1, source_target_pairs={{0,4},{2,6},{4,0},{6,2},{8,12},{10,14},{12,8},{14,10},{16,20},{18,... | collective-permute-start | bytes 3145736 | tf_op jit(solution)/shard_map/cond/branch_3_fun/ppermute | solution.py:330
  337.6 80.2 %collective-permute-start.98 = (bf16[512,2048]{1,0:T(8,128)(2,1)}, bf16[512,2048]{1,0:T(8,128)(2,1)}, u32[]{:S(2)}, u32[]{:S(2)}) collective-permute-start(bf16[512,2048]{1,0:T(8,128)(2,1)} %pad_maximum_fusion.28), channel_id=1, source_target_pairs={{0,1},{1,0},{2,3},{3,2},{4,5},{5,4},{6,7},{7,6},{8,9},{9,8},{10,11... | collective-permute-start | bytes 6291464 | tf_op jit(solution)/shard_map/cond/branch_3_fun/ppermute | solution.py:334
  365.4 54.3 %collective-permute-start.99 = (bf16[512,2048]{1,0:T(8,128)(2,1)}, bf16[512,2048]{1,0:T(8,128)(2,1)}, u32[]{:S(2)}, u32[]{:S(2)}) collective-permute-start(bf16[512,2048]{1,0:T(8,128)(2,1)} %pad_maximum_fusion.29), channel_id=1, source_target_pairs={{0,1},{1,0},{2,3},{3,2},{4,5},{5,4},{6,7},{7,6},{8,9},{9,8},{10,11... | collective-permute-start | bytes 6291464 | tf_op jit(solution)/shard_map/cond/branch_3_fun/ppermute | solution.py:334
  365.4 3.8 collective-permute-start.75
  369.2 3.7 collective-permute-start.76
  373.0 3.7 collective-permute-start.77
  376.7 3.7 collective-permute-start.78
  380.4 4.6 %collective-permute-start.79 = (f32[1,2048]{1,0:T(1,128)S(1)}, f32[1,2048]{1,0:T(1,128)S(1)}, u32[]{:S(2)}, u32[]{:S(2)}) collective-permute-start(f32[1,2048]{1,0:T(1,128)S(1)} %add.478), channel_id=1, source_target_pairs={{0,16},{2,18},{4,20},{6,22},{8,24},{10,26},{12,28},{14,30},{16,0},... | collective-permute-start | bytes 24584 | tf_op jit(solution)/shard_map/cond/branch_3_fun/ppermute | solution.py:330
  (26 other events, 237.2 us)

commit v2 on v1

v2 whole, which is shorter than its diff:
```python
import functools

import jax
import jax.numpy as jnp
from jax import lax
from jax.experimental import pallas as pl
from jax.experimental.pallas import tpu as pltpu
from jax.sharding import PartitionSpec as P

TILE = 128
ROWS = 512
SIDE = 512
OUTER = 4
CHUNKS = 2
F32 = jnp.float32
BF16 = jnp.bfloat16
BUCKETS = (60, 52, 56, 64, 68, 72)


def params(mib=60):
    return pltpu.CompilerParams(vmem_limit_bytes=mib * 1024 * 1024)


def cost(flops, moved, transcendentals=0):
    return pl.CostEstimate(flops=flops, bytes_accessed=moved, transcendentals=transcendentals)


def dot(a, b, ca, cb):
    return lax.dot_general(a, b, (((ca,), (cb,)), ((), ())), preferred_element_type=F32)


def anywhere(values):
    return [pl.BlockSpec(memory_space=pl.ANY) for _ in values]


def eye():
    row = lax.broadcasted_iota(jnp.int32, (TILE, TILE), 0)
    return row == lax.broadcasted_iota(jnp.int32, (TILE, TILE), 1)


def aligned(index, size=TILE):
    return pl.ds(pl.multiple_of(index * TILE, TILE), size)


def by_groups(first, last, one, size=4):
    groups = (last - first) // size

    def group(n, carry):
        for k in range(size):
            one(first + n * size + k)
        return carry

    def single(t, carry):
        one(t)
        return carry

    lax.fori_loop(0, groups, group, 0)
    lax.fori_loop(first + groups * size, last, single, 0)


def clear_tail(out_ref, first, last):
    def one(p):
        out_ref[aligned(p), :] = jnp.zeros((TILE, out_ref.shape[1]), out_ref.dtype)

    by_groups(first, last, one)


def pack_kernel(clusters, counts, offsets, in_ref, out_ref):
    features = in_ref.shape[1]
    for c in range(clusters):
        live = counts[c]
        start = offsets[c]

        def one(t):
            lane = t * TILE + lax.broadcasted_iota(jnp.int32, (features, TILE), 1)
            block = jnp.where(lane < live, in_ref[c, :, aligned(t)].astype(F32), 0.0)
            out_ref[aligned(start + t), :] = block.T.astype(out_ref.dtype)

        by_groups(0, offsets[c + 1] - start, one)
    clear_tail(out_ref, offsets[clusters], out_ref.shape[0] // TILE)


def pack(tiles, counts, offsets, values):
    clusters, features, nodes = values.shape
    size = tiles * TILE * features
    return pl.pallas_call(
        functools.partial(pack_kernel, clusters),
        name="pack",
        out_shape=jax.ShapeDtypeStruct((tiles * TILE, features), BF16),
        grid_spec=pltpu.PrefetchScalarGridSpec(
            num_scalar_prefetch=2,
            grid=(1,),
            in_specs=[pl.BlockSpec((clusters, features, nodes), lambda i, *_: (0, 0, 0))],
            out_specs=pl.BlockSpec((tiles * TILE, features), lambda i, *_: (0, 0)),
        ),
        compiler_params=params(),
        cost_estimate=cost(size, 4 * size),
    )(counts, offsets, values)


def unpack_kernel(counts, offsets, packed, *refs):
    out_ref = refs[-1]
    c = pl.program_id(0)
    features = out_ref.shape[1]
    live = counts[c]
    start = offsets[c]

    def one(t):
        lane = t * TILE + lax.broadcasted_iota(jnp.int32, (features, TILE), 1)
        block = packed[aligned(start + t), :].astype(F32).T
        out_ref[0, :, aligned(t)] = jnp.where(lane < live, block, 0.0)

    def clear(t):
        out_ref[0, :, aligned(t)] = jnp.zeros((features, TILE), F32)

    used = offsets[c + 1] - start
    by_groups(0, used, one)
    by_groups(used, out_ref.shape[2] // TILE, clear)


def unpack(shape, counts, offsets, packed, after=()):
    clusters, features, nodes = shape
    return pl.pallas_call(
        unpack_kernel,
        name="unpack",
        out_shape=jax.ShapeDtypeStruct(shape, F32),
        grid_spec=pltpu.PrefetchScalarGridSpec(
            num_scalar_prefetch=2,
            grid=(clusters,),
            in_specs=[pl.BlockSpec(packed.shape, lambda c, *_: (0, 0))] + anywhere(after),
            out_specs=pl.BlockSpec((1, features, nodes), lambda c, *_: (c, 0, 0)),
        ),
        compiler_params=params(),
        cost_estimate=cost(packed.size, 2 * packed.size + 4 * clusters * features * nodes),
    )(counts, offsets, packed, *after)


def adjacency_spec(nodes):
    def index(c, i, counts, offsets):
        return (c, jnp.minimum(i, (counts[c] - 1) // ROWS), 0)

    return pl.BlockSpec((1, ROWS, nodes), index)


def aggregate_kernel(clusters, counts, offsets, x_ref, a_ref, *refs):
    out_ref, masked = refs[-2:]
    c = pl.program_id(0)
    i = pl.program_id(1)
    live = counts[c]

    @pl.when(jnp.logical_and(c == 0, i == 0))
    def _():
        clear_tail(out_ref, offsets[clusters], out_ref.shape[0] // TILE)

    @pl.when(i == 0)
    def _():
        lane = lax.broadcasted_iota(jnp.int32, masked.shape, 1)
        masked[...] = jnp.where(lane < live, x_ref[0].astype(F32), 0.0).astype(BF16)

    @pl.when(i * ROWS < live)
    def _():
        total = dot(a_ref[0], masked[...], 1, 1)
        for s in range(ROWS // TILE):
            t = i * (ROWS // TILE) + s

            @pl.when(t * TILE < live)
            def _():
                block = a_ref[0, s * TILE : (s + 1) * TILE, aligned(t)]
                block = jnp.where(eye(), block.astype(F32), 0.0).astype(BF16)
                extra = dot(block, masked[:, aligned(t)], 1, 1)
                rows = total[s * TILE : (s + 1) * TILE] + extra
                out_ref[aligned(offsets[c] + t), :] = rows.astype(BF16)


def aggregate(tiles, counts, offsets, features, adjacency, after):
    clusters, width, nodes = features.shape
    return pl.pallas_call(
        functools.partial(aggregate_kernel, clusters),
        name="aggregate",
        out_shape=jax.ShapeDtypeStruct((tiles * TILE, width), BF16),
        grid_spec=pltpu.PrefetchScalarGridSpec(
            num_scalar_prefetch=2,
            grid=(clusters, nodes // ROWS),
            in_specs=[
                pl.BlockSpec((1, width, nodes), lambda c, i, *_: (c, 0, 0)),
                adjacency_spec(nodes),
                *anywhere((after,)),
            ],
            out_specs=pl.BlockSpec((tiles * TILE, width), lambda c, i, *_: (0, 0)),
            scratch_shapes=[pltpu.VMEM((width, nodes), BF16)],
        ),
        compiler_params=params(),
        cost_estimate=cost(2 * adjacency.size * width, 2 * adjacency.size),
    )(counts, offsets, features, adjacency, after)


def spread_kernel(clusters, count, counts, offsets, me, *refs):
    a_ref = refs[count]
    out_ref, packed, turned, held, sems = refs[-5:]
    c = pl.program_id(0)
    slot = lax.rem(c, 2)
    live = counts[c]
    width, nodes = turned.shape
    sizes = range(SIDE, nodes + SIDE, SIDE)

    def each(cluster, act):
        need = counts[cluster]
        for size in sizes:

            @pl.when(jnp.logical_and(need > size - SIDE, need <= size))
            def _():
                act(size)

    def copy(cluster, place, size):
        area = (slice(0, size), slice(0, size))
        return pltpu.make_async_copy(
            a_ref.at[(cluster, *area)], held.at[(place, *area)], sems.at[place]
        )

    @pl.when(c == 0)
    def _():
        each(c, lambda size: copy(c, slot, size).start())
        blocks = [(k, low, refs[low].at[k]) for low in range(count) for k in range(OUTER)]
        gather_rows(me[0], count, blocks, packed)

    @pl.when(c + 1 < clusters)
    def _():
        each(c + 1, lambda size: copy(c + 1, 1 - slot, size).start())

    start = offsets[c]
    used = offsets[c + 1] - start

    def turn(t):
        lane = t * TILE + lax.broadcasted_iota(jnp.int32, (width, TILE), 1)
        block = packed[aligned(start + t), :].astype(F32).T
        turned[:, aligned(t)] = jnp.where(lane < live, block, 0.0).astype(BF16)

    def clear(t):
        turned[:, aligned(t)] = jnp.zeros((width, TILE), BF16)

    by_groups(0, used, turn)
    by_groups(used, nodes // TILE, clear)

    def compute(size):
        copy(c, slot, size).wait()
        for j in range(0, size, SIDE):
            total = dot(turned[:, :size], held[slot, :size, j : j + SIDE], 1, 0)
            for t in range(j, j + SIDE, TILE):
                block = held[slot, t : t + TILE, t : t + TILE].astype(F32)
                diagonal = jnp.sum(jnp.where(eye(), block, 0.0), axis=0, keepdims=True)
                extra = diagonal * turned[:, t : t + TILE].astype(F32)
                lane = t + lax.broadcasted_iota(jnp.int32, (width, TILE), 1)
                value = total[:, t - j : t - j + TILE] + extra
                out_ref[0, :, t : t + TILE] = jnp.where(lane < live, value, 0.0)
        if size < nodes:
            out_ref[0, :, size:] = jnp.zeros((width, nodes - size), F32)

    each(c, compute)


def spread(counts, offsets, me, values, adjacency, after=()):
    clusters, nodes, _ = adjacency.shape
    count = len(values)
    width = values[0].shape[-1]
    return pl.pallas_call(
        functools.partial(spread_kernel, clusters, count),
        name="spread",
        out_shape=jax.ShapeDtypeStruct((clusters, width, nodes), F32),
        grid_spec=pltpu.PrefetchScalarGridSpec(
            num_scalar_prefetch=3,
            grid=(clusters,),
            in_specs=[pl.BlockSpec(values[0].shape, lambda c, *_: (0, 0, 0))] * count
            + anywhere((adjacency, *after)),
            out_specs=pl.BlockSpec((1, width, nodes), lambda c, *_: (c, 0, 0)),
            scratch_shapes=[
                pltpu.VMEM((count * values[0].size // width, width), BF16),
                pltpu.VMEM((width, nodes), BF16),
                pltpu.VMEM((2, nodes, nodes), BF16),
                pltpu.SemaphoreType.DMA((2,)),
            ],
        ),
        compiler_params=params(32),
        cost_estimate=cost(2 * adjacency.size * width, 2 * adjacency.size),
    )(counts, offsets, me, *values, adjacency, *after)


def normal(value):
    bell = jnp.exp(-0.5 * value * value)
    t = 1.0 / (1.0 + (0.3275911 * 0.5**0.5) * jnp.abs(value))
    tail = 0.5 * 1.061405429
    for term in (-1.453152027, 1.421413741, -0.284496736, 0.254829592):
        tail = tail * t + 0.5 * term
    tail = tail * t * bell
    return jnp.where(value >= 0.0, 1.0 - tail, tail), bell * 0.3989422804014327


def middle_kernel(first, which, *refs):
    refs = refs if first else refs[3:]
    agg_ref, cot_ref, w_ref, b_ref, act_ref, low_ref, bias_ref, *out_refs, held, turned = refs
    owners, rows, width = agg_ref.shape

    @pl.when(pl.program_id(0) == 0)
    def _():
        for s in range(owners):
            held[:, s * width : (s + 1) * width] = agg_ref[s]
            turned[s * width : (s + 1) * width, :] = agg_ref[s].T

    parts = cot_ref.shape[0]
    total = jnp.zeros((1, w_ref.shape[1]), F32)
    step = min(rows, TILE)
    for r in range(0, rows, step):
        pre = dot(held[r : r + step], w_ref[...], 1, 0) + b_ref[...].astype(F32)
        cdf, pdf = normal(pre)
        act = (pre * cdf).astype(BF16)
        cot = jnp.concatenate([cot_ref[k, r : r + step] for k in range(parts)], axis=1).astype(F32)
        grad = cot * (cdf + pre * pdf)
        for k in range(parts):
            act_ref[k, r : r + step] = act[:, k * width : (k + 1) * width]
        low_ref[r : r + step] = grad.astype(BF16)
        total = total + jnp.sum(grad, axis=0, keepdims=True)
    bias_ref[...] = total
    share = out_refs[0].shape[0]
    for k, out_ref in enumerate(out_refs):
        out_ref[...] = dot(turned[k * share : (k + 1) * share], low_ref[...], 1, 0).astype(out_ref.dtype)


def middle(which, dtype, agg, cot, weight, bias, before=None):
    owners, rows, width = agg.shape
    full = owners * width
    block = 256
    steps = full // 2 // block
    here = lambda g, which: (0, which[0] * steps + g)
    lead = lambda g, which: (which[0] * steps + g, 0, 0)
    begun = () if before is None else before
    return pl.pallas_call(
        functools.partial(middle_kernel, before is None),
        name="middle",
        out_shape=(
            jax.ShapeDtypeStruct((owners, rows, width), BF16),
            jax.ShapeDtypeStruct((rows, full), BF16),
            jax.ShapeDtypeStruct((1, full), F32),
        )
        + (jax.ShapeDtypeStruct((full // CHUNKS, full // 2), dtype),) * CHUNKS,
        grid_spec=pltpu.PrefetchScalarGridSpec(
            num_scalar_prefetch=1,
            grid=(steps,),
            in_specs=[pl.BlockSpec(memory_space=pl.ANY) for _ in begun]
            + [
                pl.BlockSpec((owners, rows, width), lambda g, which: (0, 0, 0)),
                pl.BlockSpec((block // width, rows, width), lead),
                pl.BlockSpec((full, block), here),
                pl.BlockSpec((1, block), here),
            ],
            out_specs=(
                pl.BlockSpec((block // width, rows, width), lead),
                pl.BlockSpec((rows, block), here),
                pl.BlockSpec((1, block), here),
            )
            + (pl.BlockSpec((full // CHUNKS, block), lambda g, which: (0, g)),) * CHUNKS,
            scratch_shapes=[pltpu.VMEM((rows, full), BF16), pltpu.VMEM((full, rows), BF16)],
        ),
        input_output_aliases={1 + k: k for k in range(len(begun))},
        compiler_params=params(),
        cost_estimate=cost(2 * rows * full * full, full * full + 8 * rows * full, rows * full),
    )(which[None], *begun, agg, cot, weight, bias[None])


def back_kernel(me, low_ref, w_ref, *refs):
    out_ref = refs[-1]
    parts, width = out_ref.shape[1], out_ref.shape[3]
    value = dot(low_ref[...], w_ref[...], 1, 1).astype(BF16)
    for k in range(parts):
        out_ref[0, k ^ (me[0] & (parts - 1))] = value[:, k * width : (k + 1) * width]


def back(me, low, weight, owners, after=()):
    rows, full = low.shape
    width = full // owners
    step = 256
    parts = step // width
    inner = owners // OUTER

    def place(i, me):
        rest = i ^ (me[0] // parts)
        return (i // (inner // parts), rest % (inner // parts), 0, 0)

    return pl.pallas_call(
        back_kernel,
        name="back",
        out_shape=jax.ShapeDtypeStruct((OUTER, inner, rows, width), BF16),
        grid_spec=pltpu.PrefetchScalarGridSpec(
            num_scalar_prefetch=1,
            grid=(full // step,),
            in_specs=[
                pl.BlockSpec((rows, full), lambda i, me: (0, 0)),
                pl.BlockSpec((step, full), lambda i, me: (i, 0)),
            ]
            + anywhere(after),
            out_specs=pl.BlockSpec((1, parts, rows, width), place),
        ),
        compiler_params=params(16),
        cost_estimate=cost(8 * rows * full * full, 8 * full * full + 16 * rows * full),
    )(me, low, weight, *after)


def split_kernel(value_ref, *refs):
    count = value_ref.shape[1]
    for j, out_ref in enumerate(refs[-count:]):
        out_ref[...] = value_ref[:, j]


def row_step(rows):
    return rows // 2 if rows % 32 == 0 else rows


def split(value, after=()):
    first, second, rows, width = value.shape
    step = row_step(rows)
    return pl.pallas_call(
        split_kernel,
        name="split",
        out_shape=[jax.ShapeDtypeStruct((first, rows, width), BF16)] * second,
        grid=(rows // step,),
        in_specs=[pl.BlockSpec((first, second, step, width), lambda i: (0, 0, i, 0))]
        + anywhere(after),
        out_specs=[pl.BlockSpec((first, step, width), lambda i: (0, i, 0))] * second,
        compiler_params=params(16),
        cost_estimate=cost(0, 4 * value.size),
    )(value, *after)


def swap_with(value, mask):
    count = lax.axis_size("feat")
    return lax.ppermute(value, "feat", [(i, i ^ mask) for i in range(count)])


def scatter(values):
    return [values[0]] + [swap_with(values[k], k) for k in range(1, len(values))]


def outer_exchange(value):
    inner = lax.axis_size("feat") // OUTER
    groups = [[k * inner + low for k in range(OUTER)] for low in range(inner)]
    return lax.all_to_all(
        value, "feat", split_axis=0, concat_axis=0, axis_index_groups=groups, tiled=True
    )


def gather_rows(me, inner, blocks, out_ref):
    for high, low, block in blocks:
        rows = block.shape[0]
        owner = high * inner + (me ^ low)
        out_ref[pl.ds(pl.multiple_of(owner * rows, 16), rows), :] = block[...]


def swap_feat(value, bit):
    return swap_with(value, 1 << bit)


def swap_rep(value):
    return lax.ppermute(value, "rep", [(0, 1), (1, 0)])


def exchange(packed):
    owners = lax.axis_size("feat")
    blocks = packed.reshape(owners, -1, packed.shape[-1])
    return lax.all_to_all(blocks, "feat", split_axis=0, concat_axis=0, tiled=True)


def place_kernel(count, where, *refs):
    out_ref = refs[-1]
    for k in range(count):

        @pl.when(pl.program_id(0) == k)
        def _():
            out_ref[...] = refs[k][...].astype(F32)


def place(where, pieces, before=None, after=()):
    count = len(pieces)
    rows, columns = pieces[0].shape
    step = min(rows, 512)
    steps = rows // step
    full = 2 * columns
    begun = () if before is None else (before,)

    def source(k):
        return lambda i, j, where: (jnp.where(i == k, j, jnp.where(i < k, 0, steps - 1)), 0)

    return pl.pallas_call(
        functools.partial(place_kernel, count),
        name="place",
        out_shape=jax.ShapeDtypeStruct((full, full), F32),
        grid_spec=pltpu.PrefetchScalarGridSpec(
            num_scalar_prefetch=1,
            grid=(count, steps),
            in_specs=[pl.BlockSpec((step, columns), source(k)) for k in range(count)]
            + anywhere(begun)
            + anywhere(after),
            out_specs=pl.BlockSpec(
                (step, columns), lambda i, j, where: (where[i] * steps + j, where[count + i])
            ),
        ),
        input_output_aliases={1 + count: 0} if begun else {},
        compiler_params=params(16),
        cost_estimate=cost(0, 6 * count * rows * columns),
    )(jnp.stack(where).astype(jnp.int32), *pieces, *begun, *after)


def halve_kernel(chunks, side, *refs):
    outs = refs[-2 * chunks :]
    for k in range(chunks):
        for part in range(2):
            kept, came = refs[4 * k + 2 * part], refs[4 * k + 2 * part + 1]
            out = outs[2 * k + part]
            out[...] = (kept[...].astype(F32) + came[...].astype(F32)).astype(out.dtype)


def halve(side, kept, came, after=()):
    chunks = len(kept)
    half, columns = kept[0].shape[0] // 2, kept[0].shape[1]
    step = min(half, 128)
    steps = half // step

    def source(k, part):
        return lambda i, side: ((side[k] if part else 1 - side[k]) * steps + i, 0)

    in_specs = []
    operands = []
    out_shape = []
    for k in range(chunks):
        for part in range(2):
            for value in (kept[k], came[k]):
                in_specs.append(pl.BlockSpec((step, columns), source(k, part)))
                operands.append(value)
        for dtype in (BF16, F32):
            out_shape.append(jax.ShapeDtypeStruct((half, columns), dtype))
    outs = pl.pallas_call(
        functools.partial(halve_kernel, chunks),
        name="halve",
        out_shape=tuple(out_shape),
        grid_spec=pltpu.PrefetchScalarGridSpec(
            num_scalar_prefetch=1,
            grid=(steps,),
            in_specs=in_specs + anywhere(after),
            out_specs=[pl.BlockSpec((step, columns), lambda i, side: (i, 0)) for _ in out_shape],
        ),
        compiler_params=params(16),
        cost_estimate=cost(2 * chunks * half * columns, 18 * chunks * half * columns),
    )(jnp.stack(side).astype(jnp.int32), *operands, *after)
    return outs[0::2], outs[1::2]


def pick_kernel(side, *refs):
    first, second = (refs[2 * k][...] + refs[2 * k + 1][...].astype(F32) for k in range(2))
    away_ref, own_ref = refs[-2:]

    @pl.when(side[0] == 0)
    def _():
        own_ref[...] = first
        away_ref[...] = second.astype(BF16)

    @pl.when(side[0] == 1)
    def _():
        own_ref[...] = second
        away_ref[...] = first.astype(BF16)


def pick(side, kept, came, after=()):
    rows, columns = kept[0].shape
    step = min(rows, 128)
    block = pl.BlockSpec((step, columns), lambda i, side: (i, 0))
    away, own = pl.pallas_call(
        pick_kernel,
        name="pick",
        out_shape=(
            jax.ShapeDtypeStruct((rows, columns), BF16),
            jax.ShapeDtypeStruct((rows, columns), F32),
        ),
        grid_spec=pltpu.PrefetchScalarGridSpec(
            num_scalar_prefetch=1,
            grid=(rows // step,),
            in_specs=[block] * 4 + anywhere(after),
            out_specs=(block, block),
        ),
        compiler_params=params(16),
        cost_estimate=cost(2 * rows * columns, 18 * rows * columns),
    )(side[None].astype(jnp.int32), kept[0], came[0], kept[1], came[1], *after)
    return [away], [own]


def sort_kernel(side, own_ref, other_ref, *refs):
    first_ref, second_ref = refs[-2:]

    @pl.when(side[0] == 0)
    def _():
        first_ref[...] = own_ref[...]
        second_ref[...] = other_ref[...]

    @pl.when(side[0] == 1)
    def _():
        first_ref[...] = other_ref[...]
        second_ref[...] = own_ref[...]


def sort(side, own, other, after=()):
    whole = pl.BlockSpec(own.shape, lambda i, side: (0, 0))
    return pl.pallas_call(
        sort_kernel,
        name="sort",
        out_shape=[jax.ShapeDtypeStruct(own.shape, BF16)] * 2,
        grid_spec=pltpu.PrefetchScalarGridSpec(
            num_scalar_prefetch=1,
            grid=(1,),
            in_specs=[whole, whole] + anywhere(after),
            out_specs=[whole, whole],
        ),
        compiler_params=params(16),
        cost_estimate=cost(0, 8 * own.size),
    )(side[None].astype(jnp.int32), own, other, *after)


def add_kernel(first_ref, second_ref, *refs):
    refs[-1][...] = first_ref[...] + second_ref[...]


def add(first, second, after=()):
    return pl.pallas_call(
        add_kernel,
        name="add",
        out_shape=jax.ShapeDtypeStruct(first.shape, F32),
        in_specs=[pl.BlockSpec(memory_space=pltpu.VMEM)] * 2 + anywhere(after),
        compiler_params=params(16),
        cost_estimate=cost(first.size, 12 * first.size),
    )(first, second, *after)


def close_kernel(chunks, *refs):
    for k in range(chunks):
        total = refs[2 * k][...] + refs[2 * k + 1][...].astype(F32)
        refs[len(refs) - chunks + k][...] = total.astype(BF16)


def close(kept, came, after=()):
    chunks = len(kept)
    pairs = [value for pair in zip(kept, came) for value in pair]
    return pl.pallas_call(
        functools.partial(close_kernel, chunks),
        name="close",
        out_shape=[jax.ShapeDtypeStruct(value.shape, BF16) for value in kept],
        in_specs=[pl.BlockSpec(memory_space=pltpu.VMEM) for _ in pairs] + anywhere(after),
        compiler_params=params(16),
        cost_estimate=cost(kept[0].size * chunks, 8 * kept[0].size * chunks),
    )(*pairs, *after)


def join_kernel(chunks, side, *refs):
    outs = refs[-chunks:]
    for k in range(chunks):
        for part in range(2):

            @pl.when(pl.program_id(0) == part)
            def _():
                outs[k][...] = refs[2 * k + part][...]


def join(side, own, other, after=()):
    chunks = len(own)
    rows, columns = own[0].shape
    step = min(rows, 256)
    steps = rows // step
    pairs = [value for pair in zip(own, other) for value in pair]

    def source(part):
        return lambda i, j, side: (jnp.where(i == part, j, 0 if part else steps - 1), 0)

    def target(k):
        return lambda i, j, side: (jnp.where(i == 0, side[k], 1 - side[k]) * steps + j, 0)

    return pl.pallas_call(
        functools.partial(join_kernel, chunks),
        name="join",
        out_shape=[jax.ShapeDtypeStruct((2 * rows, columns), BF16) for _ in own],
        grid_spec=pltpu.PrefetchScalarGridSpec(
            num_scalar_prefetch=1,
            grid=(2, steps),
            in_specs=[pl.BlockSpec((step, columns), source(n % 2)) for n in range(2 * chunks)]
            + anywhere(after),
            out_specs=[pl.BlockSpec((step, columns), target(k)) for k in range(chunks)],
        ),
        compiler_params=params(16),
        cost_estimate=cost(0, 8 * chunks * rows * columns),
    )(jnp.stack(side).astype(jnp.int32), *pairs, *after)


def run(tiles, features, adjacency, counts, offsets, weight, bias, cotangent):
    owners = lax.axis_size("feat")
    me = lax.axis_index("feat")
    core = lax.axis_index("rep")
    bits = owners.bit_length() - 1
    inner = owners // OUTER
    side = [(me >> bit) & 1 for bit in range(bits)]
    crossed = [1, 0]
    low_bits = (me & (inner - 1)).astype(jnp.int32)
    place_of = low_bits[None]

    cot = pack(tiles, counts, offsets, cotangent)
    agg = exchange(aggregate(tiles, counts, offsets, features, adjacency, cot))
    cot = exchange(cot)
    *begun, sent0, sent1 = middle(1 - core, BF16, agg, cot, weight, bias)
    came = [swap_rep(sent0), swap_rep(sent1)]
    act, low, grad_bias, *kept = middle(
        core, BF16, agg, cot, weight, bias, begun
    )

    came_bias = swap_rep(grad_bias)
    away, kept = halve(side[:2], kept, came)
    came = [swap_feat(away[k], k) for k in range(2)]
    back_rows = outer_exchange(back(place_of, low, weight, owners, away))
    grad_bias = add(grad_bias, came_bias, away)
    came_bias = swap_feat(grad_bias, 0)
    away, kept = halve([side[1], side[0]], kept, came)
    came = [swap_feat(away[k], crossed[k]) for k in range(2)]
    grad_bias = add(grad_bias, came_bias, away)
    came_bias = swap_feat(grad_bias, 1)
    away, kept = pick(side[2], kept, came, (grad_bias,))
    came = [swap_feat(away[0], 2)]
    back_rows = scatter(split(back_rows, away))
    grad_bias = add(grad_bias, came_bias, away)
    for bit in range(3, bits):
        came_bias = swap_feat(grad_bias, bit - 1)
        away, kept = halve(side[bit : bit + 1], kept, came, (grad_bias,))
        came = [swap_feat(away[0], bit)]
        grad_bias = add(grad_bias, came_bias, away)
    came_bias = swap_feat(grad_bias, bits - 1)
    grad_bias = add(grad_bias, came_bias, away)
    owned = close(kept, came, (grad_bias,))
    for bit in reversed(range(3, bits)):
        owned = join(side[bit : bit + 1], owned, [swap_feat(owned[0], bit)])
    other = swap_feat(owned[0], 2)
    grad_features = spread(counts, offsets, place_of, back_rows, adjacency, owned)
    owned = sort(side[2], owned[0], other, (grad_features,))
    other = [swap_feat(owned[k], crossed[k]) for k in range(2)]
    act, owned = lax.optimization_barrier((act, owned))
    act = exchange(act).reshape(tiles * TILE, -1)
    owned = join([side[1], side[0]], owned, other)
    across = [swap_rep(value) for value in owned]
    far = [swap_feat(owned[k], k) for k in range(2)]
    near_rows = [2 * k + side[k] for k in range(2)]
    far_rows = [2 * k + 1 - side[k] for k in range(2)]
    columns = [core] * 2 + [1 - core] * 2
    grad_weight = place(2 * near_rows + columns, [*owned, *across])
    far, grad_weight = lax.optimization_barrier((far, grad_weight))
    far_across = [swap_rep(value) for value in far]
    grad_weight = place(2 * far_rows + columns, [*far, *far_across], grad_weight)
    activations = unpack(features.shape, counts, offsets, act)
    return activations, grad_features, grad_weight, grad_bias[0]


def local(features, adjacency, counts, weight, bias, cotangent):
    features = features.transpose(1, 0, 2)
    cotangent = cotangent.transpose(1, 0, 2)
    clusters, _, nodes = features.shape
    used = (counts + TILE - 1) // TILE
    before = jnp.arange(clusters)[None] < jnp.arange(clusters + 1)[:, None]
    offsets = jnp.sum(jnp.where(before, used[None], 0), axis=1).astype(jnp.int32)
    need = offsets[-1:]
    need = jnp.maximum(need, swap_rep(need))[0]
    most = clusters * nodes // TILE
    unit = max(2, 16 * lax.axis_size("feat") // TILE)
    buckets = [b for b in BUCKETS if b < most and b % unit == 0] + [most]
    ordered = sorted(buckets)
    branch = jnp.int32(buckets.index(ordered[0]))
    for low, high in zip(ordered, ordered[1:]):
        branch = jnp.where(need > low, buckets.index(high), branch)
    branches = [functools.partial(run, b) for b in buckets]
    args = (features, adjacency, counts, offsets, weight, bias, cotangent)
    activations, grad_features, grad_weight, grad_bias = lax.switch(branch, branches, *args)
    return (
        activations.transpose(1, 0, 2),
        grad_features.transpose(1, 0, 2),
        grad_weight,
        grad_bias,
    )


def solution(mesh):
    placed = (
        P("feat", "rep", None),
        P("rep", None, None),
        P("rep"),
        P(),
        P(),
        P("feat", "rep", None),
    )
    return jax.shard_map(
        local,
        mesh=mesh,
        in_specs=placed,
        out_specs=(P("feat", "rep", None), P("feat", "rep", None), P(), P()),
        check_vma=False,
    )
```

time: 453 us -> 377 us (0.83); the launches traced: 446 us -> 382 us
  other arithmetic: 36.4 us -> 0.93 us
  waiting for transfers between devices: 206 us -> 171 us
  loops' own time: 15.2 us -> 26.5 us
  starting transfers between devices: 66.5 us -> 61.6 us
    another operation x0 -> x1, loops' own time: none -> 26.5 us  [local(): lax.switch(branch, branches, *args)]
    ppermute x20 -> x19, waiting for transfers between devices: 129 us -> 105 us  [swap_with(): return lax.ppermute(value, 'feat', [(i, i ^ mask) for i in range(count)])]
    cond x0 -> x46, local copies, waits for them, and re-layouts: none -> 17.7 us
    unnamed x1 -> x0, loops' own time: 15.2 us -> none
    unnamed x57 -> x0, local copies, waits for them, and re-layouts: 14.9 us -> none
    all_to_all x4 -> x3, waiting for transfers between devices: 73.5 us -> 60.6 us  [exchange(): lax.all_to_all(blocks, 'feat', split_axis=0, concat_axis=0, tiled=True)]
    convert_element_type x3 -> x0, other arithmetic: 11.9 us -> none  [the longest x1 11.8 us: weight_sum(): return (joined(core, own, other).astype(F32), bias_part[0])]
    add x13 -> x0, other arithmetic: 10.3 us -> none  [the longest x2 6.09 us: weight_sum(): outer(core * chunks + k, 2 * chunks, agg, low, F32) + sent[k].astype(F32)]
  transfers between devices with their start and end apart: 30 -> 31, of which waited for: 21 -> 16; matrix products, arithmetic and copies ran while one was open for 5% -> 0% of each run, Pallas kernels for 13% -> 17%
where the time goes in v2:
time: 377 us; the launch traced here: 382 us
  waiting for transfers between devices  171 us (45%)
  Pallas kernels  99.4 us (26%)
  starting transfers between devices  61.6 us (16%)
  loops' own time  26.5 us (7%)
  local copies, waits for them, and re-layouts  19 us (5%)
    ppermute x19, waiting for transfers between devices, swap_with(): return lax.ppermute(value, 'feat', [(i, i ^ mask) for i in range(count)])  105 us
    all_to_all x3, waiting for transfers between devices, exchange(): lax.all_to_all(blocks, 'feat', split_axis=0, concat_axis=0, tiled=True)  60.6 us
    another operation x1, loops' own time, local(): lax.switch(branch, branches, *args)  26.5 us
    ppermute x19, starting transfers between devices, swap_with(): return lax.ppermute(value, 'feat', [(i, i ^ mask) for i in range(count)])  25.7 us
    pallas_call x1, Pallas kernels, aggregate(): pl.pallas_call(functools.partial(aggregate_kernel, clusters), name='aggre...  24.8 us
    all_to_all x3, starting transfers between devices, exchange(): lax.all_to_all(blocks, 'feat', split_axis=0, concat_axis=0, tiled=True)  24.7 us
    pallas_call x2, Pallas kernels, middle(): pl.pallas_call(functools.partial(middle_kernel, before is None), name='mi...  23.1 us
    cond x46, local copies, waits for them, and re-layouts  17.7 us
  transfers between devices with their start and end apart: 31, of which 16 were waited for; matrix products, arithmetic and copies ran while one was open for 0% of the time, Pallas kernels for 17%

profile of v2, /device:TPU:0, one launch (start us, length us, event | category | flops | bytes accessed | tf_op | source)
XLA Modules:
  0.0 382.0 jit_solution(3410468608153831267)
XLA Ops:
  4.7 375.9 %conditional.1 = (f32[5,128,2048]{2,1,0:T(8,128)}, f32[5,128,2048]{2,1,0:T(8,128)}, f32[2048,2048]{1,0:T(8,128)}, f32[2048]{0:T(1024)}) conditional(s32[]{:T(128)} %bitcast.98, (s32[5]{0:T(128)}, s32[6]{0:T(128)S(1)}, bf16[5,128,2048]{2,1,0:T(8,128)(2,1)}, bf16[5,128,2048]{2,1,0:T(8,128)(2,1)}, ...), branch_computations={%region_1.2_spmd, %region_2.3_spmd, %region_3.4_spmd, %region_4.5_... | conditional | flops 42956357632 | bytes 520210624 | solution.py:778
  11.0 5.6 %pack.10.refs_0_ = bf16[8192,128]{1,0:T(8,128)(2,1)} custom-call(s32[5]{0:T(128)} %get-tuple-element.227.counts, s32[6]{0:T(128)S(1)} %get-tuple-element.228.offsets, bf16[5,128,2048]{2,1,0:T(8,128)(2,1)} %get-tuple-element.231.in_ref), custom_call_target="tpu_custom_call" | custom-call | flops 1048576 | bytes 4194304 | tf_op jit(solution)/shard_map/cond/branch_3_fun/pack/pallas_call | solution.py:86
  16.7 8.5 %all-to-all-start.13 = ((bf16[16,512,128]{2,1,0:T(8,128)(2,1)}), bf16[16,512,128]{2,1,0:T(8,128)(2,1)}, u32[]{:S(2)}, u32[]{:S(2)}) async-start(bf16[16,512,128]{2,1,0:T(8,128)(2,1)} %bitcast.121), calls=%async_computation.13 | async-start | bytes 4194304 | tf_op jit(solution)/shard_map/cond/branch_3_fun/all_to_all | solution.py:467
  25.1 24.8 %aggregate.10 = bf16[8192,128]{1,0:T(8,128)(2,1)} custom-call(s32[5]{0:T(128)S(1)} %copy-done.154, s32[6]{0:T(128)S(1)} %get-tuple-element.228.offsets, bf16[5,128,2048]{2,1,0:T(8,128)(2,1)S(1)} %copy-done.133, bf16[5,2048,2048]{2,1,0:T(8,128)(2,1)} %get-tuple-element.230.a_ref.refs_4_, bf16[8192,128]{1,0:T(8,128)(2,1)} %pack.10.refs_0_), custom_call_target="tpu_custom_call" | custom-call | flops 5368709120 | bytes 41943040 | tf_op jit(solution)/shard_map/cond/branch_3_fun/aggregate/pallas_call | solution.py:177
  49.9 18.3 %all-to-all-done.13.refs_1_.refs_4_ = bf16[16,512,128]{2,1,0:T(8,128)(2,1)} async-done(((bf16[16,512,128]{2,1,0:T(8,128)(2,1)}), bf16[16,512,128]{2,1,0:T(8,128)(2,1)}, u32[]{:S(2)}, u32[]{:S(2)}) %all-to-all-start.13) | async-done | bytes 2097184 | tf_op jit(solution)/shard_map/cond/branch_3_fun/all_to_all | solution.py:467
  68.3 11.3 %all-to-all-start.12 = ((bf16[16,512,128]{2,1,0:T(8,128)(2,1)}), bf16[16,512,128]{2,1,0:T(8,128)(2,1)S(1)}, u32[]{:S(2)}, u32[]{:S(2)}) async-start(bf16[16,512,128]{2,1,0:T(8,128)(2,1)} %bitcast.128), calls=%async_computation.12 | async-start | bytes 4194304 | tf_op jit(solution)/shard_map/cond/branch_3_fun/all_to_all | solution.py:467
  80.2 42.3 %all-to-all-done.12.refs_0_.refs_3_ = bf16[16,512,128]{2,1,0:T(8,128)(2,1)S(1)} async-done(((bf16[16,512,128]{2,1,0:T(8,128)(2,1)}), bf16[16,512,128]{2,1,0:T(8,128)(2,1)S(1)}, u32[]{:S(2)}, u32[]{:S(2)}) %all-to-all-start.12) | async-done | bytes 2097184 | tf_op jit(solution)/shard_map/cond/branch_3_fun/all_to_all | solution.py:467
  123.8 11.5 %middle.20 = (bf16[16,512,128]{2,1,0:T(8,128)(2,1)}, bf16[512,2048]{1,0:T(8,128)(2,1)}, f32[1,2048]{1,0:T(1,128)}, bf16[1024,1024]{1,0:T(8,128)(2,1)}, bf16[1024,1024]{1,0:T(8,128)(2,1)}) custom-call(s32[1]{0:T(128)} %bitcast.43.which, bf16[16,512,128]{2,1,0:T(8,128)(2,1)} %copy-done.138, bf16[16,512,128]{2,1,0:T(8,128)(2,1)} %all-to-all-done.13.refs_1_.refs_4_, ...), custom_call_target="tpu_custom_call" | custom-call | flops 4294967296 | bytes 12582912 | tf_op jit(solution)/shard_map/cond/branch_3_fun/middle/pallas_call | solution.py:335
  135.9 11.5 %middle.21 = (bf16[16,512,128]{2,1,0:T(8,128)(2,1)}, bf16[512,2048]{1,0:T(8,128)(2,1)}, f32[1,2048]{1,0:T(1,128)}, bf16[1024,1024]{1,0:T(8,128)(2,1)}, bf16[1024,1024]{1,0:T(8,128)(2,1)}) custom-call(s32[1]{0:T(128)} %bitcast.42.which, bf16[16,512,128]{2,1,0:T(8,128)(2,1)} %get-tuple-element.234.refs_0_, ...), custom_call_target="tpu_custom_call", output_to_operand_aliasing={{0}: (1, {}), {1}: (2, {}), {2}: (3, {})} | custom-call | flops 4294967296 | bytes 12582912 | tf_op jit(solution)/shard_map/cond/branch_3_fun/middle/pallas_call | solution.py:335
  150.6 3.5 halve.30
  156.8 9.0 %back.10 = bf16[4,4,512,128]{3,2,1,0:T(8,128)(2,1)S(1)} custom-call(s32[1]{0:T(128)} %bitcast.50.me, bf16[512,2048]{1,0:T(8,128)(2,1)S(1)} %copy-done.49, bf16[2048,2048]{1,0:T(8,128)(2,1)} %get-tuple-element.232.refs_2_.refs_5_.w_ref, bf16[512,1024]{1,0:T(8,128)(2,1)S(1)} %get-tuple-element.243.refs_0_, bf16[512,1024]{1,0:T(8,128)(2,1)S(1)} %get-tuple-element.245.refs_1_), custom_call_target="tpu_custom_call" | custom-call | flops 17179869184 | bytes 50331648 | tf_op jit(solution)/shard_map/cond/branch_3_fun/back/pallas_call | solution.py:387
  168.1 9.2 %all-to-all-start.14 = ((bf16[4,4,512,128]{3,2,1,0:T(8,128)(2,1)}), bf16[4,4,512,128]{3,2,1,0:T(8,128)(2,1)}, u32[]{:S(2)}, u32[]{:S(2)}) async-start(bf16[4,4,512,128]{3,2,1,0:T(8,128)(2,1)} %copy-done.48), calls=%async_computation.14 | async-start | bytes 4194304 | tf_op jit(solution)/shard_map/cond/branch_3_fun/all_to_all | solution.py:444
  179.7 22.6 %collective-permute-done.80.refs_1_.refs_3_ = bf16[512,1024]{1,0:T(8,128)(2,1)S(1)} collective-permute-done((bf16[512,1024]{1,0:T(8,128)(2,1)S(1)}, bf16[512,1024]{1,0:T(8,128)(2,1)S(1)}, u32[]{:S(2)}, u32[]{:S(2)}) %collective-permute-start.80) | collective-permute-done | bytes 1048608 | tf_op jit(solution)/shard_map/cond/branch_3_fun/ppermute | solution.py:434
  205.0 1.7 halve.31
  211.0 9.3 %collective-permute-done.85.second_ref = f32[1,2048]{1,0:T(1,128)S(1)} collective-permute-done((f32[1,2048]{1,0:T(1,128)S(1)}, f32[1,2048]{1,0:T(1,128)S(1)}, u32[]{:S(2)}, u32[]{:S(2)}) %collective-permute-start.85) | collective-permute-done | bytes 8224 | tf_op jit(solution)/shard_map/cond/branch_3_fun/ppermute | solution.py:434
  225.0 3.9 %collective-permute-start.86 = (bf16[256,1024]{1,0:T(8,128)(2,1)S(1)}, bf16[256,1024]{1,0:T(8,128)(2,1)S(1)}, u32[]{:S(2)}, u32[]{:S(2)}) collective-permute-start(bf16[256,1024]{1,0:T(8,128)(2,1)S(1)} %get-tuple-element.252.refs_0_), channel_id=1, source_target_pairs={{0,8},{2,10},{4,12},{6,14},{8,0},{10,2},{12,4},{14,6},{16,24},{18,... | collective-permute-start | bytes 1572872 | tf_op jit(solution)/shard_map/cond/branch_3_fun/ppermute | solution.py:434
  229.5 3.0 collective-permute-done.87.second_ref
  232.5 6.2 %collective-permute-done.86.refs_1_.refs_3_ = bf16[256,1024]{1,0:T(8,128)(2,1)S(1)} collective-permute-done((bf16[256,1024]{1,0:T(8,128)(2,1)S(1)}, bf16[256,1024]{1,0:T(8,128)(2,1)S(1)}, u32[]{:S(2)}, u32[]{:S(2)}) %collective-permute-start.86) | collective-permute-done | bytes 524320 | tf_op jit(solution)/shard_map/cond/branch_3_fun/ppermute | solution.py:434
  246.7 3.2 collective-permute-done.89.second_ref
  251.2 3.7 collective-permute-done.90.second_ref
  256.1 9.1 %collective-permute-done.91.refs_1_ = bf16[128,1024]{1,0:T(8,128)(2,1)S(1)} collective-permute-done((bf16[128,1024]{1,0:T(8,128)(2,1)S(1)}, bf16[128,1024]{1,0:T(8,128)(2,1)S(1)}, u32[]{:S(2)}, u32[]{:S(2)}) %collective-permute-start.91) | collective-permute-done | bytes 262176 | tf_op jit(solution)/shard_map/cond/branch_3_fun/ppermute | solution.py:434
  265.4 9.8 %spread.10.refs_0_ = f32[5,128,2048]{2,1,0:T(8,128)S(1)} custom-call(s32[5]{0:T(128)S(1)} %copy-done.154, s32[6]{0:T(128)S(1)} %get-tuple-element.228.offsets, s32[1]{0:T(128)} %bitcast.50.me, bf16[4,512,128]{2,1,0:T(8,128)(2,1)S(1)} %get-tuple-element.256.refs_0_, bf16[4,512,128]{2,1,0:T(8,128)(2,1)S(1)} %collective-permute-done.93.refs_1_, ...), custom_call_target="tpu_custom_call" | custom-call | flops 5368709120 | bytes 41943040 | tf_op jit(solution)/shard_map/cond/branch_3_fun/spread/pallas_call | solution.py:265
  275.3 2.2 copy-done.126
  277.6 5.0 %all-to-all-start.15 = ((bf16[16,512,128]{2,1,0:T(8,128)(2,1)}), bf16[16,512,128]{2,1,0:T(8,128)(2,1)}, u32[]{:S(2)}, u32[]{:S(2)}) async-start(bf16[16,512,128]{2,1,0:T(8,128)(2,1)} %get-tuple-element.262), calls=%async_computation.15 | async-start | bytes 4194304 | tf_op jit(solution)/shard_map/cond/branch_3_fun/all_to_all | solution.py:467
  282.6 1.9 collective-permute-start.96
  285.9 25.6 %collective-permute-done.96.refs_1_ = bf16[256,1024]{1,0:T(8,128)(2,1)S(1)} collective-permute-done((bf16[256,1024]{1,0:T(8,128)(2,1)S(1)}, bf16[256,1024]{1,0:T(8,128)(2,1)S(1)}, u32[]{:S(2)}, u32[]{:S(2)}) %collective-permute-start.96) | collective-permute-done | bytes 524320 | tf_op jit(solution)/shard_map/cond/branch_3_fun/ppermute | solution.py:434
  315.2 2.5 collective-permute-start.99
  317.8 6.0 %place.20.refs_4_ = f32[2048,2048]{1,0:T(8,128)} custom-call(s32[8]{0:T(128)S(1)} %stack.196.where, bf16[512,1024]{1,0:T(8,128)(2,1)} %get-tuple-element.265.refs_0_, bf16[512,1024]{1,0:T(8,128)(2,1)S(1)} %get-tuple-element.266.refs_1_, bf16[512,1024]{1,0:T(8,128)(2,1)} %collective-permute-done.100.refs_2_, bf16[512,1024]{1,0:T(8,128)(2,1)} %collective-permute-done.101.refs_3_), custom_call_target="tpu_custom_call" | custom-call | bytes 12582912 | tf_op jit(solution)/shard_map/cond/branch_3_fun/place/pallas_call | solution.py:490
  323.8 20.8 %collective-permute-done.98.refs_0_ = bf16[512,1024]{1,0:T(8,128)(2,1)S(1)} collective-permute-done((bf16[512,1024]{1,0:T(8,128)(2,1)}, bf16[512,1024]{1,0:T(8,128)(2,1)S(1)}, u32[]{:S(2)}, u32[]{:S(2)}) %collective-permute-start.98) | collective-permute-done | bytes 1048608 | tf_op jit(solution)/shard_map/cond/branch_3_fun/ppermute | solution.py:434
  345.2 3.5 collective-permute-done.102.refs_2_
  348.9 5.4 %place.21 = f32[2048,2048]{1,0:T(8,128)} custom-call(s32[8]{0:T(128)S(1)} %stack.194.where, bf16[512,1024]{1,0:T(8,128)(2,1)S(1)} %collective-permute-done.98.refs_0_, bf16[512,1024]{1,0:T(8,128)(2,1)S(1)} %collective-permute-done.99.refs_1_, bf16[512,1024]{1,0:T(8,128)(2,1)S(1)} %collective-permute-done.102.refs_2_, ...), custom_call_target="tpu_custom_call", output_to_operand_aliasing={{}: (5, {})} | custom-call | bytes 12582912 | tf_op jit(solution)/shard_map/cond/branch_3_fun/place/pallas_call | solution.py:490
  354.3 6.5 %unpack.10 = f32[5,128,2048]{2,1,0:T(8,128)} custom-call(s32[5]{0:T(128)S(1)} %copy-done.154, s32[6]{0:T(128)S(1)} %get-tuple-element.228.offsets, bf16[8192,128]{1,0:T(8,128)(2,1)} %bitcast.51.packed), custom_call_target="tpu_custom_call" | custom-call | flops 1048576 | bytes 7340032 | tf_op jit(solution)/shard_map/cond/branch_3_fun/unpack/pallas_call | solution.py:123
  (108 shorter events, 44.7 us)
Async XLA Ops:
  2.0 1.4 collective-permute-start.182
  16.7 51.6 %all-to-all-start.13 = ((bf16[16,512,128]{2,1,0:T(8,128)(2,1)}), bf16[16,512,128]{2,1,0:T(8,128)(2,1)}, u32[]{:S(2)}, u32[]{:S(2)}) async-start(bf16[16,512,128]{2,1,0:T(8,128)(2,1)} %bitcast.121), calls=%async_computation.13 | async-start | bytes 4194304 | tf_op jit(solution)/shard_map/cond/branch_3_fun/all_to_all | solution.py:467
  68.3 54.2 %all-to-all-start.12 = ((bf16[16,512,128]{2,1,0:T(8,128)(2,1)}), bf16[16,512,128]{2,1,0:T(8,128)(2,1)S(1)}, u32[]{:S(2)}, u32[]{:S(2)}) async-start(bf16[16,512,128]{2,1,0:T(8,128)(2,1)} %bitcast.128), calls=%async_computation.12 | async-start | bytes 4194304 | tf_op jit(solution)/shard_map/cond/branch_3_fun/all_to_all | solution.py:467
  135.3 12.1 %collective-permute-start.78 = (bf16[1024,1024]{1,0:T(8,128)(2,1)}, bf16[1024,1024]{1,0:T(8,128)(2,1)S(1)}, u32[]{:S(2)}, u32[]{:S(2)}) collective-permute-start(bf16[1024,1024]{1,0:T(8,128)(2,1)} %get-tuple-element.239), channel_id=1, source_target_pairs={{0,1},{1,0},{2,3},{3,2},{4,5},{5,4},{6,7},{7,6},{8,9},{9,8},{10,11... | collective-permute-start | bytes 6291464 | tf_op jit(solution)/shard_map/cond/branch_3_fun/ppermute | solution.py:461
  135.3 12.1 %collective-permute-start.79 = (bf16[1024,1024]{1,0:T(8,128)(2,1)}, bf16[1024,1024]{1,0:T(8,128)(2,1)}, u32[]{:S(2)}, u32[]{:S(2)}) collective-permute-start(bf16[1024,1024]{1,0:T(8,128)(2,1)} %get-tuple-element.241), channel_id=1, source_target_pairs={{0,1},{1,0},{2,3},{3,2},{4,5},{5,4},{6,7},{7,6},{8,9},{9,8},{10,11... | collective-permute-start | bytes 6291464 | tf_op jit(solution)/shard_map/cond/branch_3_fun/ppermute | solution.py:461
  168.1 35.3 %copy-start.13 = (f32[512,1024]{1,0:T(8,128)S(1)}, f32[512,1024]{1,0:T(8,128)}, u32[]{:S(2)}) copy-start(f32[512,1024]{1,0:T(8,128)} %copy-done.12) | copy-start | bytes 6291460 | tf_op jit(solution)/shard_map/cond
  168.1 72.0 %all-to-all-start.14 = ((bf16[4,4,512,128]{3,2,1,0:T(8,128)(2,1)}), bf16[4,4,512,128]{3,2,1,0:T(8,128)(2,1)}, u32[]{:S(2)}, u32[]{:S(2)}) async-start(bf16[4,4,512,128]{3,2,1,0:T(8,128)(2,1)} %copy-done.48), calls=%async_computation.14 | async-start | bytes 4194304 | tf_op jit(solution)/shard_map/cond/branch_3_fun/all_to_all | solution.py:444
  177.4 24.9 %collective-permute-start.80 = (bf16[512,1024]{1,0:T(8,128)(2,1)S(1)}, bf16[512,1024]{1,0:T(8,128)(2,1)S(1)}, u32[]{:S(2)}, u32[]{:S(2)}) collective-permute-start(bf16[512,1024]{1,0:T(8,128)(2,1)S(1)} %get-tuple-element.243.refs_0_), channel_id=1, source_target_pairs={{0,2},{2,0},{4,6},{6,4},{8,10},{10,8},{12,14},{14,12},{16,18},{18,... | collective-permute-start | bytes 3145736 | tf_op jit(solution)/shard_map/cond/branch_3_fun/ppermute | solution.py:434
  178.7 24.8 %collective-permute-start.81 = (bf16[512,1024]{1,0:T(8,128)(2,1)}, bf16[512,1024]{1,0:T(8,128)(2,1)S(1)}, u32[]{:S(2)}, u32[]{:S(2)}) collective-permute-start(bf16[512,1024]{1,0:T(8,128)(2,1)} %copy-done.62), channel_id=1, source_target_pairs={{0,4},{2,6},{4,0},{6,2},{8,12},{10,14},{12,8},{14,10},{16,20},{18,... | collective-permute-start | bytes 3145736 | tf_op jit(solution)/shard_map/cond/branch_3_fun/ppermute | solution.py:434
  206.8 13.6 %collective-permute-start.82 = (bf16[256,1024]{1,0:T(8,128)(2,1)}, bf16[256,1024]{1,0:T(8,128)(2,1)S(1)}, u32[]{:S(2)}, u32[]{:S(2)}) collective-permute-start(bf16[256,1024]{1,0:T(8,128)(2,1)} %get-tuple-element.247.refs_0_), channel_id=1, source_target_pairs={{0,4},{2,6},{4,0},{6,2},{8,12},{10,14},{12,8},{14,10},{16,20},{18,... | collective-permute-start | bytes 1572872 | tf_op jit(solution)/shard_map/cond/branch_3_fun/ppermute | solution.py:434
  207.7 12.6 %collective-permute-start.83 = (bf16[256,1024]{1,0:T(8,128)(2,1)}, bf16[256,1024]{1,0:T(8,128)(2,1)S(1)}, u32[]{:S(2)}, u32[]{:S(2)}) collective-permute-start(bf16[256,1024]{1,0:T(8,128)(2,1)} %get-tuple-element.249.refs_1_), channel_id=1, source_target_pairs={{0,2},{2,0},{4,6},{6,4},{8,10},{10,8},{12,14},{14,12},{16,18},{18,... | collective-permute-start | bytes 1572872 | tf_op jit(solution)/shard_map/cond/branch_3_fun/ppermute | solution.py:434
  208.9 1.2 collective-permute-start.84
  210.1 10.3 %collective-permute-start.85 = (f32[1,2048]{1,0:T(1,128)S(1)}, f32[1,2048]{1,0:T(1,128)S(1)}, u32[]{:S(2)}, u32[]{:S(2)}) collective-permute-start(f32[1,2048]{1,0:T(1,128)S(1)} %add.104.first_ref), channel_id=1, source_target_pairs={{0,2},{2,0},{4,6},{6,4},{8,10},{10,8},{12,14},{14,12},{16,18},{18,... | collective-permute-start | bytes 24584 | tf_op jit(solution)/shard_map/cond/branch_3_fun/ppermute | solution.py:434
  225.0 13.8 %collective-permute-start.86 = (bf16[256,1024]{1,0:T(8,128)(2,1)S(1)}, bf16[256,1024]{1,0:T(8,128)(2,1)S(1)}, u32[]{:S(2)}, u32[]{:S(2)}) collective-permute-start(bf16[256,1024]{1,0:T(8,128)(2,1)S(1)} %get-tuple-element.252.refs_0_), channel_id=1, source_target_pairs={{0,8},{2,10},{4,12},{6,14},{8,0},{10,2},{12,4},{14,6},{16,24},{18,... | collective-permute-start | bytes 1572872 | tf_op jit(solution)/shard_map/cond/branch_3_fun/ppermute | solution.py:434
  228.9 3.7 collective-permute-start.87
  238.9 16.1 %collective-permute-start.88 = (bf16[128,1024]{1,0:T(8,128)(2,1)S(1)}, bf16[128,1024]{1,0:T(8,128)(2,1)S(1)}, u32[]{:S(2)}, u32[]{:S(2)}) collective-permute-start(bf16[128,1024]{1,0:T(8,128)(2,1)S(1)} %get-tuple-element.254.refs_0_), channel_id=1, source_target_pairs={{0,16},{2,18},{4,20},{6,22},{8,24},{10,26},{12,28},{14,30},{16,0},... | collective-permute-start | bytes 786440 | tf_op jit(solution)/shard_map/cond/branch_3_fun/ppermute | solution.py:434
  241.9 23.5 %collective-permute-start.93 = (bf16[4,512,128]{2,1,0:T(8,128)(2,1)S(1)}, bf16[4,512,128]{2,1,0:T(8,128)(2,1)S(1)}, u32[]{:S(2)}, u32[]{:S(2)}) collective-permute-start(bf16[4,512,128]{2,1,0:T(8,128)(2,1)S(1)} %get-tuple-element.257), channel_id=1, source_target_pairs={{0,2},{2,0},{4,6},{6,4},{8,10},{10,8},{12,14},{14,12},{16,18},{18,... | collective-permute-start | bytes 1572872 | tf_op jit(solution)/shard_map/cond/branch_3_fun/ppermute | solution.py:434
  242.7 22.7 %collective-permute-start.94 = (bf16[4,512,128]{2,1,0:T(8,128)(2,1)S(1)}, bf16[4,512,128]{2,1,0:T(8,128)(2,1)S(1)}, u32[]{:S(2)}, u32[]{:S(2)}) collective-permute-start(bf16[4,512,128]{2,1,0:T(8,128)(2,1)S(1)} %get-tuple-element.258), channel_id=1, source_target_pairs={{0,4},{2,6},{4,0},{6,2},{8,12},{10,14},{12,8},{14,10},{16,20},{18,... | collective-permute-start | bytes 1572872 | tf_op jit(solution)/shard_map/cond/branch_3_fun/ppermute | solution.py:434
  244.4 21.0 %collective-permute-start.95 = (bf16[4,512,128]{2,1,0:T(8,128)(2,1)S(1)}, bf16[4,512,128]{2,1,0:T(8,128)(2,1)S(1)}, u32[]{:S(2)}, u32[]{:S(2)}) collective-permute-start(bf16[4,512,128]{2,1,0:T(8,128)(2,1)S(1)} %get-tuple-element.259), channel_id=1, source_target_pairs={{0,6},{2,4},{4,2},{6,0},{8,14},{10,12},{12,10},{14,8},{16,22},{18,... | collective-permute-start | bytes 1572872 | tf_op jit(solution)/shard_map/cond/branch_3_fun/ppermute | solution.py:434
  245.4 4.4 %collective-permute-start.89 = (f32[1,2048]{1,0:T(1,128)S(1)}, f32[1,2048]{1,0:T(1,128)S(1)}, u32[]{:S(2)}, u32[]{:S(2)}) collective-permute-start(f32[1,2048]{1,0:T(1,128)S(1)} %add.106.refs_4_.first_ref), channel_id=1, source_target_pairs={{0,8},{2,10},{4,12},{6,14},{8,0},{10,2},{12,4},{14,6},{16,24},{18,... | collective-permute-start | bytes 24584 | tf_op jit(solution)/shard_map/cond/branch_3_fun/ppermute | solution.py:434
  249.9 5.0 %collective-permute-start.90 = (f32[1,2048]{1,0:T(1,128)S(1)}, f32[1,2048]{1,0:T(1,128)S(1)}, u32[]{:S(2)}, u32[]{:S(2)}) collective-permute-start(f32[1,2048]{1,0:T(1,128)S(1)} %add.107.first_ref), channel_id=1, source_target_pairs={{0,16},{2,18},{4,20},{6,22},{8,24},{10,26},{12,28},{14,30},{16,0},... | collective-permute-start | bytes 24584 | tf_op jit(solution)/shard_map/cond/branch_3_fun/ppermute | solution.py:434
  255.0 10.2 %collective-permute-start.91 = (bf16[128,1024]{1,0:T(8,128)(2,1)S(1)}, bf16[128,1024]{1,0:T(8,128)(2,1)S(1)}, u32[]{:S(2)}, u32[]{:S(2)}) collective-permute-start(bf16[128,1024]{1,0:T(8,128)(2,1)S(1)} %close.10.refs_0_), channel_id=1, source_target_pairs={{0,16},{2,18},{4,20},{6,22},{8,24},{10,26},{12,28},{14,30},{16,0},... | collective-permute-start | bytes 786440 | tf_op jit(solution)/shard_map/cond/branch_3_fun/ppermute | solution.py:434
  265.3 9.9 %collective-permute-start.92 = (bf16[256,1024]{1,0:T(8,128)(2,1)S(1)}, bf16[256,1024]{1,0:T(8,128)(2,1)S(1)}, u32[]{:S(2)}, u32[]{:S(2)}) collective-permute-start(bf16[256,1024]{1,0:T(8,128)(2,1)S(1)} %join.20.refs_5_.own_ref), channel_id=1, source_target_pairs={{0,8},{2,10},{4,12},{6,14},{8,0},{10,2},{12,4},{14,6},{16,24},{18,... | collective-permute-start | bytes 1572872 | tf_op jit(solution)/shard_map/cond/branch_3_fun/ppermute | solution.py:434
  277.6 76.7 %all-to-all-start.15 = ((bf16[16,512,128]{2,1,0:T(8,128)(2,1)}), bf16[16,512,128]{2,1,0:T(8,128)(2,1)}, u32[]{:S(2)}, u32[]{:S(2)}) async-start(bf16[16,512,128]{2,1,0:T(8,128)(2,1)} %get-tuple-element.262), calls=%async_computation.15 | async-start | bytes 4194304 | tf_op jit(solution)/shard_map/cond/branch_3_fun/all_to_all | solution.py:467
  282.6 29.0 %collective-permute-start.96 = (bf16[256,1024]{1,0:T(8,128)(2,1)S(1)}, bf16[256,1024]{1,0:T(8,128)(2,1)S(1)}, u32[]{:S(2)}, u32[]{:S(2)}) collective-permute-start(bf16[256,1024]{1,0:T(8,128)(2,1)S(1)} %get-tuple-element.263.refs_0_), channel_id=1, source_target_pairs={{0,4},{2,6},{4,0},{6,2},{8,12},{10,14},{12,8},{14,10},{16,20},{18,... | collective-permute-start | bytes 1572872 | tf_op jit(solution)/shard_map/cond/branch_3_fun/ppermute | solution.py:434
  284.4 27.1 %collective-permute-start.97 = (bf16[256,1024]{1,0:T(8,128)(2,1)S(1)}, bf16[256,1024]{1,0:T(8,128)(2,1)S(1)}, u32[]{:S(2)}, u32[]{:S(2)}) collective-permute-start(bf16[256,1024]{1,0:T(8,128)(2,1)S(1)} %get-tuple-element.264.refs_2_), channel_id=1, source_target_pairs={{0,2},{2,0},{4,6},{6,4},{8,10},{10,8},{12,14},{14,12},{16,18},{18,... | collective-permute-start | bytes 1572872 | tf_op jit(solution)/shard_map/cond/branch_3_fun/ppermute | solution.py:434
  313.2 4.6 %collective-permute-start.100 = (bf16[512,1024]{1,0:T(8,128)(2,1)}, bf16[512,1024]{1,0:T(8,128)(2,1)}, u32[]{:S(2)}, u32[]{:S(2)}) collective-permute-start(bf16[512,1024]{1,0:T(8,128)(2,1)} %get-tuple-element.265.refs_0_), channel_id=1, source_target_pairs={{0,1},{1,0},{2,3},{3,2},{4,5},{5,4},{6,7},{7,6},{8,9},{9,8},{10,11... | collective-permute-start | bytes 3145736 | tf_op jit(solution)/shard_map/cond/branch_3_fun/ppermute | solution.py:461
  313.2 4.6 %collective-permute-start.101 = (bf16[512,1024]{1,0:T(8,128)(2,1)S(1)}, bf16[512,1024]{1,0:T(8,128)(2,1)}, u32[]{:S(2)}, u32[]{:S(2)}) collective-permute-start(bf16[512,1024]{1,0:T(8,128)(2,1)S(1)} %get-tuple-element.266.refs_1_), channel_id=1, source_target_pairs={{0,1},{1,0},{2,3},{3,2},{4,5},{5,4},{6,7},{7,6},{8,9},{9,8},{10,11... | collective-permute-start | bytes 3145736 | tf_op jit(solution)/shard_map/cond/branch_3_fun/ppermute | solution.py:461
  313.7 30.9 %collective-permute-start.98 = (bf16[512,1024]{1,0:T(8,128)(2,1)}, bf16[512,1024]{1,0:T(8,128)(2,1)S(1)}, u32[]{:S(2)}, u32[]{:S(2)}) collective-permute-start(bf16[512,1024]{1,0:T(8,128)(2,1)} %get-tuple-element.265.refs_0_), channel_id=1, source_target_pairs={{0,2},{2,0},{4,6},{6,4},{8,10},{10,8},{12,14},{14,12},{16,18},{18,... | collective-permute-start | bytes 3145736 | tf_op jit(solution)/shard_map/cond/branch_3_fun/ppermute | solution.py:434
  315.2 29.4 %collective-permute-start.99 = (bf16[512,1024]{1,0:T(8,128)(2,1)S(1)}, bf16[512,1024]{1,0:T(8,128)(2,1)S(1)}, u32[]{:S(2)}, u32[]{:S(2)}) collective-permute-start(bf16[512,1024]{1,0:T(8,128)(2,1)S(1)} %get-tuple-element.266.refs_1_), channel_id=1, source_target_pairs={{0,4},{2,6},{4,0},{6,2},{8,12},{10,14},{12,8},{14,10},{16,20},{18,... | collective-permute-start | bytes 3145736 | tf_op jit(solution)/shard_map/cond/branch_3_fun/ppermute | solution.py:434
  344.6 4.1 %collective-permute-start.102 = (bf16[512,1024]{1,0:T(8,128)(2,1)S(1)}, bf16[512,1024]{1,0:T(8,128)(2,1)S(1)}, u32[]{:S(2)}, u32[]{:S(2)}) collective-permute-start(bf16[512,1024]{1,0:T(8,128)(2,1)S(1)} %collective-permute-done.98.refs_0_), channel_id=1, source_target_pairs={{0,1},{1,0},{2,3},{3,2},{4,5},{5,4},{6,7},{7,6},{8,9},{9,8},{10,11... | collective-permute-start | bytes 3145736 | tf_op jit(solution)/shard_map/cond/branch_3_fun/ppermute | solution.py:461
  344.6 4.3 %collective-permute-start.103 = (bf16[512,1024]{1,0:T(8,128)(2,1)S(1)}, bf16[512,1024]{1,0:T(8,128)(2,1)}, u32[]{:S(2)}, u32[]{:S(2)}) collective-permute-start(bf16[512,1024]{1,0:T(8,128)(2,1)S(1)} %collective-permute-done.99.refs_1_), channel_id=1, source_target_pairs={{0,1},{1,0},{2,3},{3,2},{4,5},{5,4},{6,7},{7,6},{8,9},{9,8},{10,11... | collective-permute-start | bytes 3145736 | tf_op jit(solution)/shard_map/cond/branch_3_fun/ppermute | solution.py:461
  (22 other events, 88.1 us)
